TPU v7x, 256 devices: a whole 4x4x8 slice. The times are simulated.
256 devices in a mesh: blk: 128 (over z, x_lo, y, core), seg: 2 (over x_hi).
Axes of the slice: x: 4 (x_hi: 2, x_lo: 2; x = x_hi * 2 + x_lo), y: 4, z: 8, core: 2. Of those that a mesh axis runs over, the one named last changes fastest.
Arguments:
- spectra: bfloat16 [8, 8192, 2, 2048], P('seg', 'blk'), may hold values from -3000 to 3000
- owner_device: int32 [524288, 1], P('blk'), may hold values from 0 to 127; in each aligned block of 4096 rows (0 to 4095, 4096 to 8191, ...) at most 64 rows name the same one
- stack_slot: int32 [524288], P('blk'), may hold values from 0 to 127
Outputs:
- stacks: bfloat16 [16384, 512], P('blk', 'seg')
Inputs may be any that keep to these rules, and one draw needn't show every extreme that they name: `owner_device`: among the 4096 rows of one block and round (aligned blocks of rows) at most 64 name the same owner, and exactly 64 in some of them.
All inputs are finite; a program needn't handle non-finite values.
Results may differ from a plain program's by a relative error of at most 0.0034.
Values may be sent and summed in bfloat16 or wider, within the bound.
A program may use at most 64 MiB of HBM per device.

v0:
```python
import math

import jax
import jax.numpy as jnp
from jax import lax
from jax.sharding import PartitionSpec as P

F = 2048
NFFT = 16384
LAGS = 512
WBAND = 128
STACKS_DEV = 128


def shifted(value, axis, steps):
    count = lax.axis_size(axis)
    initial, last = (max(0, -steps), min(count, count - steps))
    return lax.ppermute(value, axis, [(source, source + steps) for source in range(initial, last)])


def whiten(spectra):
    seg_count, chan_count, part_count, freq_count = spectra.shape
    values = spectra.astype(jnp.float32).reshape(
        seg_count, chan_count, part_count, freq_count // WBAND, WBAND
    )
    power_mean = jnp.mean(values * values, axis=(2, 4), keepdims=True)
    scaled = values * lax.rsqrt(power_mean + 1e-06)
    return scaled.reshape(seg_count, chan_count, part_count, freq_count).astype(jnp.bfloat16)


def lag_table(first_bin, bin_count, lag_first, lag_count, factor):
    bin_numbers = first_bin + lax.iota(jnp.int32, bin_count) + 1
    lag_steps = lag_first + lax.iota(jnp.int32, lag_count) - LAGS // 2
    wrapped = jnp.mod(bin_numbers[:, None] * lag_steps[None, :], NFFT)
    phases = wrapped.astype(jnp.float32) * (2.0 * math.pi / NFFT)
    both = jnp.concatenate([jnp.cos(phases), -jnp.sin(phases)], axis=0) * factor
    return both.astype(jnp.bfloat16)


def half_stack(partner, own_block):
    chan_count = own_block.shape[1]
    bin_count = own_block.shape[3]
    real_part = jnp.sum(
        partner[:, :, None, 0, :] * own_block[:, None, :, 0, :]
        + partner[:, :, None, 1, :] * own_block[:, None, :, 1, :],
        axis=0,
    )
    imag_part = jnp.sum(
        partner[:, :, None, 1, :] * own_block[:, None, :, 0, :]
        - partner[:, :, None, 0, :] * own_block[:, None, :, 1, :],
        axis=0,
    )
    joined = jnp.concatenate(
        [
            real_part.reshape(chan_count * chan_count, bin_count),
            imag_part.reshape(chan_count * chan_count, bin_count),
        ],
        axis=1,
    )
    return joined.astype(jnp.bfloat16)


def project(partner, own_block, groups, lag_first, lag_count, factor):
    seg_count, chan_count, part_count, freq_count = own_block.shape
    per_group = seg_count // groups
    bin_count = min(128, freq_count)

    def freq_step(position, running):
        first_bin = position * bin_count
        partner_bins = lax.dynamic_slice_in_dim(partner, first_bin, bin_count, 3).astype(
            jnp.float32
        )
        own_bins = lax.dynamic_slice_in_dim(own_block, first_bin, bin_count, 3).astype(jnp.float32)
        bin_table = lag_table(first_bin, bin_count, lag_first, lag_count, factor)
        for seg_group in range(groups):
            first_seg = seg_group * per_group
            stacked = half_stack(
                partner_bins[first_seg : first_seg + per_group],
                own_bins[first_seg : first_seg + per_group],
            )
            running = running + jnp.dot(stacked, bin_table, preferred_element_type=jnp.float32)
        return running

    initial = jnp.zeros((chan_count * chan_count, lag_count), jnp.float32)
    return lax.fori_loop(0, freq_count // bin_count, freq_step, initial)


def local(spectra, owner_device, stack_slot):
    whitened = whiten(spectra)
    seg_devices = lax.axis_size("seg")
    blk_devices = lax.axis_size("blk")
    pair_rows = spectra.shape[1] * spectra.shape[1]
    factor = (2.0 * F * spectra.shape[0] * seg_devices) ** (-0.5)
    lag_share = LAGS // seg_devices
    capacity = max(8, 2 * pair_rows // blk_devices)
    source_side = lax.all_gather(whitened, "seg", axis=0, tiled=True)
    partner = shifted(source_side, "blk", 1)
    tile_half = project(
        partner, source_side, seg_devices, lax.axis_index("seg") * lag_share, lag_share, factor
    )
    tile_rows = tile_half.astype(jnp.bfloat16)
    owner_rows = owner_device[0:pair_rows, 0]
    owner_hot = (owner_rows[:, None] == lax.iota(jnp.int32, blk_devices)[None, :]).astype(jnp.int32)
    position = jnp.sum((jnp.cumsum(owner_hot, axis=0) - owner_hot) * owner_hot, axis=1)
    destination = owner_rows * capacity + position
    outgoing = (
        jnp.zeros((blk_devices * capacity, lag_share), jnp.bfloat16).at[destination].set(tile_rows)
    )
    outgoing_slot = (
        jnp.full((blk_devices * capacity, 1), -1, jnp.int32).at[destination, 0].set(stack_slot)
    )
    received = lax.all_to_all(outgoing, "blk", split_axis=0, concat_axis=0, tiled=True)
    received_slot = lax.all_to_all(outgoing_slot, "blk", split_axis=0, concat_axis=0, tiled=True)
    one_hot = (lax.iota(jnp.int32, STACKS_DEV)[:, None] == received_slot[:, 0][None, :]).astype(
        jnp.bfloat16
    )
    stacks = jnp.dot(one_hot, received, preferred_element_type=jnp.float32)
    return stacks.astype(jnp.bfloat16)


def solution(mesh):
    placed = (P("seg", "blk", None, None), P("blk", None), P("blk"))
    return jax.shard_map(
        local, mesh=mesh, in_specs=placed, out_specs=P("blk", "seg"), check_vma=False
    )
```

profile of v0, /device:TPU:4, one launch (start us, length us, event | category | flops | bytes accessed | tf_op | source)
XLA Modules:
  0.0 518.0 jit_solution(4598334419325242202)
XLA Ops:
  15.2 4.1 fusion.20
  19.3 63.7 %all-gather.2.cloned.1.call-done = bf16[8,64,2,2048]{3,1,2,0:T(8,128)(2,1)} async-done(((bf16[4,64,2,2048]{3,1,2,0:T(8,128)(2,1)}), bf16[8,64,2,2048]{3,1,2,0:T(8,128)(2,1)}) %all-gather.2.cloned.1.call-update) | async-done | bytes 4194320 | tf_op jit(solution)/shard_map/all_gather | solution.py:96
  90.3 15.7 %scatter_custom_fusion.1 = s32[8192]{0:T(1024)S(1)} fusion(s32[4096]{0:T(1024)S(1)} %broadcast_select_fusion, s32[4096]{0:T(1024)} %param.7, s32[]{:T(128)} %constant.122.clone.1), kind=kCustom, calls=%fused_computation.73 | custom fusion | bytes 33280
  106.7 13.2 %all-to-all-start = ((s32[128,64,1]{1,2,0:T(1,128)}), s32[128,64,1]{1,2,0:T(1,128)S(1)}, u32[]{:S(2)}, u32[]{:S(2)}) async-start(s32[128,64,1]{1,2,0:T(1,128)} %bitcast.6), calls=%async_computation | async-start | bytes 131072 | tf_op jit(solution)/shard_map/all_to_all | solution.py:113
  120.0 242.1 %while.16 = (s32[]{:T(128)}, f32[4096,256]{1,0:T(8,128)}, bf16[8,64,2,2048]{3,1,2,0:T(8,128)(2,1)}, bf16[8,64,2,2048]{3,1,2,0:T(8,128)(2,1)}, s32[]{:T(128)}, /*index=5*/s32[]{:T(128)}, s32[]{:T(128)}, s32[]{:T(128)}, s32[]{:T(128)}) while((s32[]{:T(128)}, f32[4096,256]{1,0:T(8,128)}, bf16[8,64,2,2048]{3,1,2,0:T(8,128)(2,1)}, ...), condition=%wide.region_11.12_spmd.clone, body=%wide.region_6.11_spmd.clone.sunk | while | flops 1117881088 | bytes 31722664 | solution.py:85
  121.3 3.9 add_reduce_fusion.4
  134.3 3.9 add_reduce_fusion.4
  149.6 3.9 add_reduce_fusion.4
  164.9 3.9 add_reduce_fusion.4
  180.1 3.9 add_reduce_fusion.4
  195.4 3.9 add_reduce_fusion.4
  210.7 3.9 add_reduce_fusion.4
  225.9 3.9 add_reduce_fusion.4
  241.2 3.9 add_reduce_fusion.4
  256.5 3.9 add_reduce_fusion.4
  271.7 3.9 add_reduce_fusion.4
  287.0 3.9 add_reduce_fusion.4
  302.2 3.9 add_reduce_fusion.4
  317.5 3.9 add_reduce_fusion.4
  332.8 3.9 add_reduce_fusion.4
  348.0 3.9 add_reduce_fusion.4
  362.0 20.9 %scatter_custom_fusion = bf16[8192,256]{1,0:T(8,128)(2,1)} fusion(s32[4096]{0:T(1024)S(1)} %bitcast.68, f32[4096,256]{1,0:T(8,128)} %get-tuple-element.139, bf16[]{:T(256)} %constant.126.clone.1), kind=kCustom, calls=%fused_computation.56 | custom fusion | flops 1048576 | bytes 8388610 | tf_op jit(solution)/shard_map/scatter | solution.py:107
  383.0 28.5 %all-to-all-start.1 = ((bf16[128,64,256]{2,1,0:T(8,128)(2,1)}), bf16[128,64,256]{2,1,0:T(8,128)(2,1)}, u32[]{:S(2)}, u32[]{:S(2)}) async-start(bf16[128,64,256]{2,1,0:T(8,128)(2,1)} %bitcast.63), calls=%async_computation.1 | async-start | bytes 8388608 | tf_op jit(solution)/shard_map/all_to_all | solution.py:112
  412.9 94.7 %all-to-all-done.1 = bf16[128,64,256]{2,1,0:T(8,128)(2,1)} async-done(((bf16[128,64,256]{2,1,0:T(8,128)(2,1)}), bf16[128,64,256]{2,1,0:T(8,128)(2,1)}, u32[]{:S(2)}, u32[]{:S(2)}) %all-to-all-start.1) | async-done | bytes 4194336 | tf_op jit(solution)/shard_map/all_to_all | solution.py:112
  (213 shorter events, 200.0 us)
Async XLA Ops:
  6.5 76.5 %all-gather.2.cloned.1.call-start = ((), (), s32[]{:S(2)}) async-start(), calls=%async_computation.2 | async-start | bytes 6291456 | tf_op jit(solution)/shard_map/all_gather | solution.py:96
  9.8 5.3 %copy-start = (bf16[4,64,2,2048]{3,2,1,0:T(2,128)(2,1)S(1)}, bf16[4,64,2,2048]{3,2,1,0:T(2,128)(2,1)}, u32[]{:S(2)}) copy-start(bf16[4,64,2,2048]{3,2,1,0:T(2,128)(2,1)} %param.5) | copy-start | bytes 6291460
  15.2 71.1 %copy-start.1 = (s32[4096,1]{0,1:T(1,128)S(1)}, s32[4096,1]{0,1:T(1,128)}, u32[]{:S(2)}) copy-start(s32[4096,1]{0,1:T(1,128)} %param.6) | copy-start | bytes 49156
  83.0 36.9 %collective-permute-start = (bf16[8,64,2,2048]{3,1,2,0:T(8,128)(2,1)}, bf16[8,64,2,2048]{3,1,2,0:T(8,128)(2,1)}, u32[]{:S(2)}, u32[]{:S(2)}) collective-permute-start(bf16[8,64,2,2048]{3,1,2,0:T(8,128)(2,1)} %all-gather.2.cloned.1.call-done), channel_id=1, source_target_pairs={{0,2},{2,4},{4,6},{6,8},{8,10},{10,12},{12,14},{14,16},{16,18},{18... | collective-permute-start | bytes 12582920 | tf_op jit(solution)/shard_map/ppermute | solution.py:18
  87.3 2.7 copy-start.2
  87.3 2.8 copy-start.3
  106.7 276.2 %all-to-all-start = ((s32[128,64,1]{1,2,0:T(1,128)}), s32[128,64,1]{1,2,0:T(1,128)S(1)}, u32[]{:S(2)}, u32[]{:S(2)}) async-start(s32[128,64,1]{1,2,0:T(1,128)} %bitcast.6), calls=%async_computation | async-start | bytes 131072 | tf_op jit(solution)/shard_map/all_to_all | solution.py:113
  383.0 124.7 %all-to-all-start.1 = ((bf16[128,64,256]{2,1,0:T(8,128)(2,1)}), bf16[128,64,256]{2,1,0:T(8,128)(2,1)}, u32[]{:S(2)}, u32[]{:S(2)}) async-start(bf16[128,64,256]{2,1,0:T(8,128)(2,1)} %bitcast.63), calls=%async_computation.1 | async-start | bytes 8388608 | tf_op jit(solution)/shard_map/all_to_all | solution.py:112
Sparse Core Ops, SparseCore 0:
  19.4 63.5 all-gather.1
where the time goes:
time: 522 us; the launch traced here: 518 us
  other arithmetic  167 us (32%)
  waiting for transfers between devices  158 us (30%)
  matrix products  90.7 us (17%)
  starting transfers between devices  45 us (9%)
  local copies, waits for them, and re-layouts  41.7 us (8%)
  between operations  13.6 us (3%)
    reduce_sum x32, other arithmetic, half_stack(): jnp.sum(partner[:, :, None, 0, :] * own_block[:, None, :, 0, :] + partner...  124 us
    all_to_all x1, waiting for transfers between devices, local(): lax.all_to_all(outgoing, 'blk', split_axis=0, concat_axis=0, tiled=True)  94.7 us
    dot_general x32, matrix products, freq_step(): jnp.dot(stacked, bin_table, preferred_element_type=jnp.float32)  87.2 us
    all_gather x1, waiting for transfers between devices, local(): source_side = lax.all_gather(whitened, 'seg', axis=0, tiled=True)  63.7 us
    all_to_all x1, starting transfers between devices, local(): lax.all_to_all(outgoing, 'blk', split_axis=0, concat_axis=0, tiled=True)  28.5 us
    scatter x1, other arithmetic, local(): jnp.zeros((blk_devices * capacity, lag_share), jnp.bfloat16).at[destination]  20.9 us
    dynamic_slice x16, local copies, waits for them, and re-layouts, freq_step(): lax.dynamic_slice_in_dim(own_block, first_bin, bin_count, 3)  17.2 us
    unnamed x10, local copies, waits for them, and re-layouts  16.1 us
  transfers between devices with their start and end apart: 4, of which 2 were waited for; matrix products, arithmetic and copies ran while one was open for 55% of the time, Pallas kernels for 0%

commit v1 on v0

v1 whole, which is shorter than its diff:
```python
import functools
import math

import jax
import jax.numpy as jnp
import numpy as np
from jax import lax
from jax.experimental import pallas as pl
from jax.experimental.pallas import tpu as pltpu
from jax.sharding import PartitionSpec as P

F = 2048
NFFT = 16384
LAGS = 512
HALF = LAGS // 2
WBAND = 128
STACKS_DEV = 128
CB = 64
SEGS = 8
PAIRS = CB * CB
CAP = 64
GROUP = 16
GROUPS = F // GROUP
WIDE = 128
VMEM = pl.BlockSpec(memory_space=pltpu.VMEM)
SMEM = pl.BlockSpec(memory_space=pltpu.SMEM)


def lag_rows(factor):
    bins = np.arange(1, F + 1)

    def phases(lags):
        wrapped = (np.asarray(lags)[:, None] * bins[None, :]) % NFFT
        return wrapped.astype(np.float32) * np.float32(2.0 * math.pi / NFFT)

    scale = np.float32(factor)
    last = np.zeros((16, F), np.float32)
    last[0] = np.cos(phases([HALF]))[0] * scale
    cos_rows = np.concatenate([np.cos(phases(np.arange(HALF))) * scale, last])
    sin_rows = np.sin(phases(np.concatenate([[HALF], np.arange(1, HALF)]))) * scale
    return cos_rows.astype(jnp.bfloat16), sin_rows.astype(jnp.bfloat16)


def whiten_kernel(x_ref, o_ref):
    lane = lax.broadcasted_iota(jnp.int32, (CB, WIDE), 1) // GROUP
    for band in range(F // WBAND):
        parts = []
        for part in range(2):
            first = part * F + band * WBAND
            parts.append([x_ref[s, :, first : first + WBAND].astype(jnp.float32) for s in range(4)])
        values = []
        scales = []
        for s in range(4):
            power = jnp.sum(parts[0][s] * parts[0][s] + parts[1][s] * parts[1][s], axis=1, keepdims=True)
            scales.append(lax.rsqrt(power * (1.0 / (2 * WBAND)) + 1e-06))
        for part in range(2):
            for s in range(4):
                values.append(parts[part][s] * scales[s])
        for step in (1, 2, 4):
            low = (lane // step) % 2 == 0
            swapped = list(values)
            for q in range(8):
                if q & step:
                    continue
                a, b = values[q], values[q + step]
                swapped[q] = jnp.where(low, a, pltpu.roll(b, GROUP * step, 1))
                swapped[q + step] = jnp.where(low, pltpu.roll(a, WIDE - GROUP * step, 1), b)
            values = swapped
        for g in range(8):
            first = (band * 8 + g) * WIDE
            o_ref[:, first : first + WIDE] = values[g].astype(jnp.bfloat16)


def whiten(spectra):
    return pl.pallas_call(
        whiten_kernel,
        out_shape=jax.ShapeDtypeStruct((CB, GROUPS * WIDE), jnp.bfloat16),
        in_specs=[VMEM],
        out_specs=VMEM,
        compiler_params=pltpu.CompilerParams(vmem_limit_bytes=40 * 2**20),
        cost_estimate=pl.CostEstimate(flops=20_000_000, bytes_accessed=2**22, transcendentals=4096),
        name="whiten",
    )(spectra.reshape(4, CB, 2 * F))


def tile_kernel(chans, sign_ref, p_ref, o_ref, cos_ref, sin_ref, keep_ref, send_ref, g_re, g_im):
    unroll = 4
    row = lax.broadcasted_iota(jnp.int32, (GROUP, WIDE), 0)
    lane = lax.broadcasted_iota(jnp.int32, (GROUP, WIDE), 1)
    mask = jnp.where(row == lane % GROUP, 1.0, 0.0).astype(jnp.bfloat16)
    wide_lane = lax.broadcasted_iota(jnp.int32, (CB, WIDE), 1)
    turn = jnp.where(wide_lane < WIDE // 2, -1.0, 1.0).astype(jnp.bfloat16)
    zero = jnp.zeros((CB, WIDE), jnp.bfloat16)

    def one(group):
        cols = pl.ds(pl.multiple_of(group * WIDE, WIDE), WIDE)
        own = o_ref[:, cols]
        turned = jnp.concatenate([own[:, WIDE // 2 :], own[:, : WIDE // 2]], axis=1) * turn
        right = jnp.concatenate(
            [
                jnp.concatenate([own, zero], 1),
                jnp.concatenate([zero, own], 1),
                jnp.concatenate([turned, zero], 1),
                jnp.concatenate([zero, turned], 1),
            ],
            0,
        )
        spread = jnp.broadcast_to(p_ref[:, cols][:, None, :], (chans, GROUP, WIDE)) * mask[None]
        spread = spread.reshape(chans // 2, 2, GROUP, WIDE)
        left = jnp.concatenate([spread[:, 0], spread[:, 1]], axis=2).reshape(chans * 8, 2 * WIDE)
        out = lax.dot_general(
            left, right, (((1,), (1,)), ((), ())), preferred_element_type=jnp.float32
        ).astype(jnp.bfloat16)
        rows = pl.ds(pl.multiple_of(group * GROUP, GROUP), GROUP)
        for i in range(chans // 2):
            g_re[rows, i * WIDE : (i + 1) * WIDE] = out[i * GROUP : (i + 1) * GROUP, :WIDE]
            g_im[rows, i * WIDE : (i + 1) * WIDE] = out[i * GROUP : (i + 1) * GROUP, WIDE:]

    def body(i, carry):
        for u in range(unroll):
            one(i * unroll + u)
        return carry

    lax.fori_loop(0, GROUPS // unroll, body, 0)
    sign = sign_ref[0]
    top = lax.broadcasted_iota(jnp.int32, (HALF, 256), 0) == 0
    for j in range(chans * CB // 256):
        cols = slice(j * 256, (j + 1) * 256)
        even = jnp.dot(cos_ref[...], g_re[:, cols], preferred_element_type=jnp.float32)
        odd = jnp.dot(sin_ref[...], g_im[:, cols], preferred_element_type=jnp.float32)
        low, last = even[:HALF], even[HALF : HALF + 1]
        behind = jnp.where(top, last, low) + odd
        ahead = jnp.where(top, low, low - odd)
        keep_ref[:, cols] = jnp.where(sign > 0, behind, ahead)
        send_ref[:, cols] = jnp.where(sign > 0, ahead, behind).astype(jnp.bfloat16)


def tile_halves(chans, sign, partner, own, cos_rows, sin_rows):
    pairs = chans * CB
    return pl.pallas_call(
        functools.partial(tile_kernel, chans),
        out_shape=(
            jax.ShapeDtypeStruct((HALF, pairs), jnp.float32),
            jax.ShapeDtypeStruct((HALF, pairs), jnp.bfloat16),
        ),
        in_specs=[SMEM, VMEM, VMEM, VMEM, VMEM],
        out_specs=(VMEM, VMEM),
        scratch_shapes=[pltpu.VMEM((F, pairs), jnp.bfloat16)] * 2,
        compiler_params=pltpu.CompilerParams(vmem_limit_bytes=56 * 2**20),
        cost_estimate=pl.CostEstimate(
            flops=25_000_000_000 * chans // CB, bytes_accessed=2**23, transcendentals=0
        ),
        name="tiles",
    )(sign, partner, own, cos_rows, sin_rows)


def place_kernel(chunks, dest_ref, *refs):
    keeps, gots = refs[:chunks], refs[chunks : 2 * chunks]
    out_ref, rows, spread = refs[2 * chunks :]
    pairs = PAIRS // chunks
    for chunk in range(chunks):
        for j in range(pairs // 256):
            cols = slice(j * 256, (j + 1) * 256)
            total = keeps[chunk][:, cols] + gots[chunk][:, cols].astype(jnp.float32)
            first = chunk * pairs + j * 256
            rows[first : first + 256, :] = total.T

    def clear(i, carry):
        spread[pl.ds(pl.multiple_of(i * 64, 64), 64), :] = jnp.zeros((64, HALF), jnp.float32)
        return carry

    lax.fori_loop(0, spread.shape[0] // 64, clear, 0)

    def move(i, carry):
        for u in range(16):
            p = i * 16 + u
            spread[pl.ds(dest_ref[p], 1), :] = rows[pl.ds(p, 1), :]
        return carry

    lax.fori_loop(0, PAIRS // 16, move, 0)

    def finish(i, carry):
        at = pl.ds(pl.multiple_of(i * 64, 64), 64)
        out_ref[at, :] = spread[at, :].astype(jnp.bfloat16)
        return carry

    lax.fori_loop(0, spread.shape[0] // 64, finish, 0)


def place_rows(dest, keeps, gots, rows_out):
    chunks = len(keeps)
    return pl.pallas_call(
        functools.partial(place_kernel, chunks),
        out_shape=jax.ShapeDtypeStruct((rows_out, HALF), jnp.bfloat16),
        in_specs=[SMEM] + [VMEM] * (2 * chunks),
        out_specs=VMEM,
        scratch_shapes=[
            pltpu.VMEM((PAIRS, HALF), jnp.float32),
            pltpu.VMEM((rows_out, HALF), jnp.float32),
        ],
        compiler_params=pltpu.CompilerParams(vmem_limit_bytes=56 * 2**20),
        name="place",
    )(dest, *keeps, *gots)


def local(spectra, owner_device, stack_slot):
    blk_devices = lax.axis_size("blk")
    seg = lax.axis_index("seg")
    factor = (2.0 * F * SEGS) ** (-0.5)
    cos_rows, sin_rows = lag_rows(factor)
    chunks = 2
    chans = CB // chunks
    whitened = whiten(spectra)
    ahead = [(b, b + 1) for b in range(blk_devices - 1)]
    partners = [
        lax.ppermute(whitened[i * chans : (i + 1) * chans], "blk", ahead) for i in range(chunks)
    ]
    sign = jnp.where(seg == 0, 1, -1).astype(jnp.int32).reshape(1)
    keeps, gots = [], []
    for partner in partners:
        keep, send = tile_halves(chans, sign, partner, whitened, cos_rows, sin_rows)
        keeps.append(keep)
        gots.append(lax.ppermute(send, "seg", [(0, 1), (1, 0)]))

    owner_rows = owner_device[:, 0]
    owner_hot = (owner_rows[:, None] == lax.iota(jnp.int32, blk_devices)[None, :]).astype(jnp.int32)
    position = jnp.sum((jnp.cumsum(owner_hot, axis=0) - owner_hot) * owner_hot, axis=1)
    destination = owner_rows * CAP + position
    outgoing = place_rows(destination, keeps, gots, blk_devices * CAP)
    outgoing_slot = (
        jnp.full((blk_devices * CAP, 1), -1, jnp.int32).at[destination, 0].set(stack_slot)
    )
    received = lax.all_to_all(outgoing, "blk", split_axis=0, concat_axis=0, tiled=True)
    received_slot = lax.all_to_all(outgoing_slot, "blk", split_axis=0, concat_axis=0, tiled=True)
    one_hot = (lax.iota(jnp.int32, STACKS_DEV)[:, None] == received_slot[:, 0][None, :]).astype(
        jnp.bfloat16
    )
    stacks = jnp.dot(one_hot, received, preferred_element_type=jnp.float32)
    lags = lax.iota(jnp.int32, HALF)
    turned = jnp.roll(stacks[:, ::-1], 1, axis=1)
    stacks = jnp.where(seg == 0, turned, stacks)
    return stacks.astype(jnp.bfloat16)


def solution(mesh):
    placed = (P("seg", "blk", None, None), P("blk", None), P("blk"))
    return jax.shard_map(
        local, mesh=mesh, in_specs=placed, out_specs=P("blk", "seg"), check_vma=False
    )
```

time: 522 us -> 245 us (0.47)
  other arithmetic: 167 us -> 4.73 us
  matrix products: 90.7 us -> 2.9 us
  Pallas kernels: 0 us -> 70 us
  waiting for transfers between devices: 158 us -> 94.7 us
  local copies, waits for them, and re-layouts: 41.7 us -> 27.9 us
  between operations: 13.6 us -> 0.2 us
    reduce_sum x34 -> x0, other arithmetic: 128 us -> none  [the longest x32 124 us: half_stack(): jnp.sum(partner[:, :, None, 0, :] * own_block[:, None, :, 0, :] + partner...]
    dot_general x32 -> x0, matrix products: 87.2 us -> none  [freq_step(): jnp.dot(stacked, bin_table, preferred_element_type=jnp.float32)]
    pallas_call x0 -> x4, Pallas kernels: none -> 70 us  [the longest x2 43.2 us: tile_halves(): pl.pallas_call(functools.partial(tile_kernel, chans), out_shape=(jax.Shap...]
    all_gather x1 -> x0, waiting for transfers between devices: 63.7 us -> none  [local(): source_side = lax.all_gather(whitened, 'seg', axis=0, tiled=True)]
    scatter x1 -> x0, other arithmetic: 20.9 us -> none  [local(): jnp.zeros((blk_devices * capacity, lag_share), jnp.bfloat16).at[destination]]
    dynamic_slice x16 -> x0, local copies, waits for them, and re-layouts: 17.2 us -> none  [freq_step(): lax.dynamic_slice_in_dim(own_block, first_bin, bin_count, 3)]
    all_to_all x1, starting transfers between devices: 28.5 us -> 12.8 us  [local(): lax.all_to_all(outgoing, 'blk', split_axis=0, concat_axis=0, tiled=True)]
    cos x16 -> x0, other arithmetic: 9.51 us -> none  [lag_table(): both = jnp.concatenate([jnp.cos(phases), -jnp.sin(phases)], axis=0) * factor]
  transfers between devices with their start and end apart: 4 -> 6, of which waited for: 2 -> 1; matrix products, arithmetic and copies ran while one was open for 55% -> 9% of each run, Pallas kernels for 0% -> 27%
where the time goes in v1:
time: 245 us; the launch traced here: 244 us
  waiting for transfers between devices  94.7 us (39%)
  Pallas kernels  70 us (29%)
  starting transfers between devices  43.9 us (18%)
  local copies, waits for them, and re-layouts  27.9 us (11%)
  other arithmetic  4.73 us (2%)
  matrix products  2.9 us (1%)
    all_to_all x1, waiting for transfers between devices, local(): lax.all_to_all(outgoing, 'blk', split_axis=0, concat_axis=0, tiled=True)  94.7 us
    pallas_call x2, Pallas kernels, tile_halves(): pl.pallas_call(functools.partial(tile_kernel, chans), out_shape=(jax.Shap...  43.2 us
    pallas_call x1, Pallas kernels, place_rows(): pl.pallas_call(functools.partial(place_kernel, chunks), out_shape=jax.Sha...  21.7 us
    all_to_all x1, starting transfers between devices, local(): lax.all_to_all(outgoing_slot, 'blk', split_axis=0, concat_axis=0, tiled=T...  21.1 us
    unnamed x17, local copies, waits for them, and re-layouts  19.4 us
    all_to_all x1, starting transfers between devices, local(): lax.all_to_all(outgoing, 'blk', split_axis=0, concat_axis=0, tiled=True)  12.8 us
    ppermute x2, starting transfers between devices, local(): lax.ppermute(whitened[i * chans:(i + 1) * chans], 'blk', ahead)  6.49 us
    pallas_call x1, Pallas kernels, whiten(): pl.pallas_call(whiten_kernel, out_shape=jax.ShapeDtypeStruct((CB, GROUPS...  5.1 us
  transfers between devices with their start and end apart: 6, of which 1 were waited for; matrix products, arithmetic and copies ran while one was open for 9% of the time, Pallas kernels for 27%

profile of v1, /device:TPU:4, one launch (start us, length us, event | category | flops | bytes accessed | tf_op | source)
XLA Modules:
  0.0 244.4 jit_solution(17548112623929043759)
XLA Ops:
  0.0 4.5 %reshape.31.x_ref = bf16[4,64,4096]{2,1,0:T(8,128)(2,1)} reshape(bf16[4,64,2,2048]{3,2,1,0:T(2,128)(2,1)} %param.5) | data formatting | bytes 4194304 | tf_op jit(solution)/shard_map/reshape | solution.py:83
  4.5 1.6 copy-done.1
  6.1 5.1 %whiten.1.o_ref = bf16[64,16384]{1,0:T(8,128)(2,1)S(1)} custom-call(bf16[4,64,4096]{2,1,0:T(8,128)(2,1)S(1)} %copy-done.1), custom_call_target="tpu_custom_call" | custom-call | flops 20000000 | bytes 4194304 | tf_op jit(solution)/shard_map/whiten/pallas_call | solution.py:75
  11.2 1.3 fusion.11
  12.9 2.7 %collective-permute-start = (bf16[32,16384]{1,0:T(8,128)(2,1)}, bf16[32,16384]{1,0:T(8,128)(2,1)}, u32[]{:S(2)}, u32[]{:S(2)}) collective-permute-start(bf16[32,16384]{1,0:T(8,128)(2,1)} %get-tuple-element.14), channel_id=1, source_target_pairs={{0,2},{2,4},{4,6},{6,8},{8,10},{10,12},{12,14},{14,16},{16,18},{18... | collective-permute-start | bytes 3145736 | tf_op jit(solution)/shard_map/ppermute | solution.py:216
  15.6 3.8 %collective-permute-start.1 = (bf16[32,16384]{1,0:T(8,128)(2,1)S(1)}, bf16[32,16384]{1,0:T(8,128)(2,1)}, u32[]{:S(2)}, u32[]{:S(2)}) collective-permute-start(bf16[32,16384]{1,0:T(8,128)(2,1)S(1)} %get-tuple-element.13), channel_id=1, source_target_pairs={{0,2},{2,4},{4,6},{6,8},{8,10},{10,12},{12,14},{14,16},{16,18},{18... | collective-permute-start | bytes 3145736 | tf_op jit(solution)/shard_map/ppermute | solution.py:216
  19.5 0.6 fusion.4
  20.4 1.2 copy.10
  21.6 1.4 fusion.2
  23.1 21.6 %tiles.2 = (f32[256,2048]{1,0:T(8,128)}, bf16[256,2048]{1,0:T(8,128)(2,1)}) custom-call(s32[1]{0:T(128)} %bitcast.7.sign_ref, bf16[32,16384]{1,0:T(8,128)(2,1)} %collective-permute-done.p_ref, bf16[64,16384]{1,0:T(8,128)(2,1)} %copy-done, bf16[272,2048]{1,0:T(8,128)(2,1)} %constant.7.clone.cos_ref, bf16[256,2048]{1,0:T(8,128)(2,1)} %constant.26.clone.sin_ref), custom_call_target="tpu_custom_call" | custom-call | flops 12499999744 | bytes 8388608 | tf_op jit(solution)/shard_map/tiles/pallas_call | solution.py:140
  45.2 21.6 %tiles.3 = (f32[256,2048]{1,0:T(8,128)}, bf16[256,2048]{1,0:T(8,128)(2,1)}) custom-call(s32[1]{0:T(128)} %bitcast.7.sign_ref, bf16[32,16384]{1,0:T(8,128)(2,1)} %collective-permute-done.1.p_ref, bf16[64,16384]{1,0:T(8,128)(2,1)} %copy-done, bf16[272,2048]{1,0:T(8,128)(2,1)} %constant.7.clone.cos_ref, bf16[256,2048]{1,0:T(8,128)(2,1)} %constant.26.clone.sin_ref), custom_call_target="tpu_custom_call" | custom-call | flops 12499999744 | bytes 8388608 | tf_op jit(solution)/shard_map/tiles/pallas_call | solution.py:140
  66.8 3.0 %collective-permute-start.3 = (bf16[256,2048]{1,0:T(8,128)(2,1)}, bf16[256,2048]{1,0:T(8,128)(2,1)S(1)}, u32[]{:S(2)}, u32[]{:S(2)}) collective-permute-start(bf16[256,2048]{1,0:T(8,128)(2,1)} %get-tuple-element.12), channel_id=1, source_target_pairs={{0,1},{1,0},{2,3},{3,2},{4,5},{5,4},{6,7},{7,6},{8,9},{9,8},{10,11... | collective-permute-start | bytes 3145736 | tf_op jit(solution)/shard_map/ppermute | solution.py:223
  70.1 15.7 %scatter_custom_fusion = s32[8192]{0:T(1024)S(1)} fusion(s32[4096]{0:T(1024)S(1)} %broadcast_select_fusion, s32[4096]{0:T(1024)} %param.7, s32[]{:T(128)} %constant.10.clone.1), kind=kCustom, calls=%fused_computation.20 | custom fusion | bytes 33280
  85.8 0.7 all_to_all.14
  86.5 21.1 %all-to-all-start = ((s32[128,64,1]{1,2,0:T(1,128)}), s32[128,64,1]{1,2,0:T(1,128)S(1)}, u32[]{:S(2)}, u32[]{:S(2)}) async-start(s32[128,64,1]{1,2,0:T(1,128)} %bitcast.6), calls=%async_computation | async-start | bytes 131072 | tf_op jit(solution)/shard_map/all_to_all | solution.py:234
  107.7 0.6 multiply_add_fusion.dest_ref
  108.3 1.0 copy-done.2
  109.7 21.7 %place.1 = bf16[8192,256]{1,0:T(8,128)(2,1)} custom-call(s32[4096]{0:T(1024)} %multiply_add_fusion.dest_ref, f32[256,2048]{1,0:T(8,128)} %get-tuple-element.9.refs_0_, f32[256,2048]{1,0:T(8,128)} %get-tuple-element.10.refs_1_, bf16[256,2048]{1,0:T(8,128)(2,1)} %copy-done.2, bf16[256,2048]{1,0:T(8,128)(2,1)} %copy-done.3), custom_call_target="tpu_custom_call" | custom-call | tf_op jit(solution)/shard_map/place/pallas_call | solution.py:192
  131.4 12.8 %all-to-all-start.1 = ((bf16[128,64,256]{2,1,0:T(8,128)(2,1)}), bf16[128,64,256]{2,1,0:T(8,128)(2,1)}, u32[]{:S(2)}, u32[]{:S(2)}) async-start(bf16[128,64,256]{2,1,0:T(8,128)(2,1)} %bitcast.20), calls=%async_computation.1 | async-start | bytes 8388608 | tf_op jit(solution)/shard_map/all_to_all | solution.py:233
  144.2 0.5 broadcast.41
  144.7 0.8 reduce.7
  145.6 94.7 %all-to-all-done.1 = bf16[128,64,256]{2,1,0:T(8,128)(2,1)} async-done(((bf16[128,64,256]{2,1,0:T(8,128)(2,1)}), bf16[128,64,256]{2,1,0:T(8,128)(2,1)}, u32[]{:S(2)}, u32[]{:S(2)}) %all-to-all-start.1) | async-done | bytes 4194336 | tf_op jit(solution)/shard_map/all_to_all | solution.py:233
  240.3 2.9 %fusion = bf16[128,256]{1,0:T(8,128)(2,1)S(1)} fusion(bf16[8192,256]{1,0:T(8,128)(2,1)} %bitcast.9, s32[8192]{0:T(1024)S(1)} %eq.54), kind=kOutput, calls=%fused_computation.2 | convolution fusion | flops 537919488 | bytes 4292608 | tf_op jit(solution)/shard_map/dot_general | solution.py:238
  243.6 0.7 fusion.7
  (32 shorter events, 2.5 us)
Async XLA Ops:
  4.5 1.6 copy-start.1
  11.2 1.7 copy-start
  11.2 8.2 %copy-start.4 = (s32[4096,1]{0,1:T(1,128)S(1)}, s32[4096,1]{0,1:T(1,128)}, u32[]{:S(2)}) copy-start(s32[4096,1]{0,1:T(1,128)} %param.6) | copy-start | bytes 49156
  12.9 10.2 %collective-permute-start = (bf16[32,16384]{1,0:T(8,128)(2,1)}, bf16[32,16384]{1,0:T(8,128)(2,1)}, u32[]{:S(2)}, u32[]{:S(2)}) collective-permute-start(bf16[32,16384]{1,0:T(8,128)(2,1)} %get-tuple-element.14), channel_id=1, source_target_pairs={{0,2},{2,4},{4,6},{6,8},{8,10},{10,12},{12,14},{14,16},{16,18},{18... | collective-permute-start | bytes 3145736 | tf_op jit(solution)/shard_map/ppermute | solution.py:216
  15.6 29.6 %collective-permute-start.1 = (bf16[32,16384]{1,0:T(8,128)(2,1)S(1)}, bf16[32,16384]{1,0:T(8,128)(2,1)}, u32[]{:S(2)}, u32[]{:S(2)}) collective-permute-start(bf16[32,16384]{1,0:T(8,128)(2,1)S(1)} %get-tuple-element.13), channel_id=1, source_target_pairs={{0,2},{2,4},{4,6},{6,8},{8,10},{10,12},{12,14},{14,16},{16,18},{18... | collective-permute-start | bytes 3145736 | tf_op jit(solution)/shard_map/ppermute | solution.py:216
  44.6 25.2 %copy-start.5 = (s32[2]{0:T(128)S(1)}, s32[2]{0:T(128)}, u32[]{:S(2)}) copy-start(s32[2]{0:T(128)} %constant.30) | copy-start | bytes 28
  44.7 25.3 %copy-start.6 = (s32[2]{0:T(128)S(1)}, s32[2]{0:T(128)}, u32[]{:S(2)}) copy-start(s32[2]{0:T(128)} %constant.33) | copy-start | bytes 28
  44.7 63.6 %collective-permute-start.2 = (bf16[256,2048]{1,0:T(8,128)(2,1)}, bf16[256,2048]{1,0:T(8,128)(2,1)S(1)}, u32[]{:S(2)}, u32[]{:S(2)}) collective-permute-start(bf16[256,2048]{1,0:T(8,128)(2,1)} %get-tuple-element.11), channel_id=1, source_target_pairs={{0,1},{1,0},{2,3},{3,2},{4,5},{5,4},{6,7},{7,6},{8,9},{9,8},{10,11... | collective-permute-start | bytes 3145736 | tf_op jit(solution)/shard_map/ppermute | solution.py:223
  66.8 41.5 %collective-permute-start.3 = (bf16[256,2048]{1,0:T(8,128)(2,1)}, bf16[256,2048]{1,0:T(8,128)(2,1)S(1)}, u32[]{:S(2)}, u32[]{:S(2)}) collective-permute-start(bf16[256,2048]{1,0:T(8,128)(2,1)} %get-tuple-element.12), channel_id=1, source_target_pairs={{0,1},{1,0},{2,3},{3,2},{4,5},{5,4},{6,7},{7,6},{8,9},{9,8},{10,11... | collective-permute-start | bytes 3145736 | tf_op jit(solution)/shard_map/ppermute | solution.py:223
  86.5 44.9 %all-to-all-start = ((s32[128,64,1]{1,2,0:T(1,128)}), s32[128,64,1]{1,2,0:T(1,128)S(1)}, u32[]{:S(2)}, u32[]{:S(2)}) async-start(s32[128,64,1]{1,2,0:T(1,128)} %bitcast.6), calls=%async_computation | async-start | bytes 131072 | tf_op jit(solution)/shard_map/all_to_all | solution.py:234
  108.3 1.0 copy-start.2
  108.3 1.4 copy-start.3
  131.4 108.9 %all-to-all-start.1 = ((bf16[128,64,256]{2,1,0:T(8,128)(2,1)}), bf16[128,64,256]{2,1,0:T(8,128)(2,1)}, u32[]{:S(2)}, u32[]{:S(2)}) async-start(bf16[128,64,256]{2,1,0:T(8,128)(2,1)} %bitcast.20), calls=%async_computation.1 | async-start | bytes 8388608 | tf_op jit(solution)/shard_map/all_to_all | solution.py:233

commit v2 on v1

--- a/solution.py
+++ b/solution.py
@@ -203,6 +203,180 @@
     )(dest, *keeps, *gots)
 
 
+SLOTS_A, SLOTS_C, SLOTS_B = 48, 48, 32
+AC = SLOTS_A + SLOTS_C
+
+
+def place_of(z, x, y, core):
+    return ((z * 2 + x) * 4 + y) * 2 + core
+
+
+def reduce_kernel(
+    rows_ref, slots_ref, out_ref,
+    sib_rows, sib_slots, da, db, dc, ra, rb, rc, sa, sb, sc, ra2, rb2, rc2, t, tb, rt, rtb,
+    send_sem, recv_sem,
+):
+    blk = lax.axis_index("blk")
+    seg = lax.axis_index("seg")
+    core = blk % 2
+    y = (blk // 2) % 4
+    x = (blk // 8) % 2
+    z = blk // 16
+    other = (place_of(z, x, y, 1 - core), seg)
+    across = (place_of(z, 1 - x, y, core), seg)
+
+    def along_y(k):
+        return (place_of(z, x, (y + k) % 4, core), seg)
+
+    def along_z(k):
+        return (place_of((z + k) % 8, x, y, core), seg)
+
+    partners = [other, across] + [along_y(k) for k in (1, 2, 3)] + [along_z(k) for k in range(1, 8)]
+    barrier = pltpu.get_barrier_semaphore()
+    for partner in partners:
+        pl.semaphore_signal(barrier, inc=1, device_id=partner, device_id_type=pl.DeviceIdType.MESH)
+    pl.semaphore_wait(barrier, len(partners))
+    used = [0]
+
+    def copy(src, dst, device):
+        i = used[0]
+        used[0] += 1
+        made = pltpu.make_async_remote_copy(
+            src_ref=src, dst_ref=dst, send_sem=send_sem.at[i], recv_sem=recv_sem.at[i],
+            device_id=device, device_id_type=pl.DeviceIdType.MESH,
+        )
+        made.start()
+        return made
+
+    half = CB * CAP
+    copies = [
+        copy(rows_ref.at[pl.ds((1 - core) * half, half)], sib_rows, other),
+        copy(slots_ref.at[pl.ds((1 - core) * CB, CB)], sib_slots, other),
+    ]
+    for made in copies:
+        made.wait()
+    lane = lax.broadcasted_iota(jnp.int32, (1, STACKS_DEV), 1)
+    slot = lax.broadcasted_iota(jnp.int32, (STACKS_DEV, STACKS_DEV), 0)
+
+    def dense(i, carry):
+        zz, xx, yy = i // 8, (i // 4) % 2, i % 4
+        names = jnp.where(
+            lane < CAP, slots_ref[pl.ds(core * CB + i, 1), :], sib_slots[pl.ds(i, 1), :]
+        )
+        hot = jnp.where(slot == names, 1.0, 0.0).astype(jnp.bfloat16)
+        mine = rows_ref[pl.ds(pl.multiple_of(core * half + i * CAP, CAP), CAP), :]
+        theirs = sib_rows[pl.ds(pl.multiple_of(i * CAP, CAP), CAP), :]
+        total = jnp.dot(
+            hot, jnp.concatenate([mine, theirs], 0), preferred_element_type=jnp.float32
+        ).astype(jnp.bfloat16)
+        da[yy, zz * 2 + xx] = total[:SLOTS_A]
+        dc[xx, zz * 4 + yy] = total[SLOTS_A:AC]
+        db[zz, xx * 4 + yy] = total[AC:]
+        return carry
+
+    lax.fori_loop(0, CB, dense, 0)
+    first_c = [copy(dc.at[1 - x], rc, across)]
+    first_a = [copy(da.at[(y + k) % 4], ra.at[k - 1], along_y(k)) for k in (1, 2, 3)]
+    first_b = [copy(db.at[(z + k) % 8], rb.at[k - 1], along_z(k)) for k in range(1, 8)]
+    copies = first_c + first_a + first_b
+
+    def wide(value):
+        return value.astype(jnp.float32)
+
+    for made in first_c:
+        made.wait()
+
+    def sum_c(i, carry):
+        total = wide(dc[x, i]) + wide(rc[i])
+        sc[i % 4, i // 4] = total.astype(jnp.bfloat16)
+        return carry
+
+    lax.fori_loop(0, 32, sum_c, 0)
+    second_c = [copy(sc.at[(y + k) % 4], rc2.at[k - 1], along_y(k)) for k in (1, 2, 3)]
+    for made in first_a:
+        made.wait()
+
+    def sum_a(i, carry):
+        total = wide(da[y, i])
+        for k in range(3):
+            total += wide(ra[k, i])
+        sa[i % 2, i // 2] = total.astype(jnp.bfloat16)
+        return carry
+
+    lax.fori_loop(0, 16, sum_a, 0)
+    second_a = [copy(sa.at[1 - x], ra2, across)]
+    for made in first_b:
+        made.wait()
+
+    def sum_b(i, carry):
+        total = wide(db[z, i])
+        for k in range(7):
+            total += wide(rb[k, i])
+        sb[i % 4, i // 4] = total.astype(jnp.bfloat16)
+        return carry
+
+    lax.fori_loop(0, 8, sum_b, 0)
+    second_b = [copy(sb.at[(y + k) % 4], rb2.at[k - 1], along_y(k)) for k in (1, 2, 3)]
+    for made in second_a + second_c:
+        made.wait()
+
+    def sum_ac(i, carry):
+        t[i, :SLOTS_A] = (wide(sa[x, i]) + wide(ra2[i])).astype(jnp.bfloat16)
+        total = wide(sc[y, i])
+        for k in range(3):
+            total += wide(rc2[k, i])
+        t[i, SLOTS_A:] = total.astype(jnp.bfloat16)
+        return carry
+
+    lax.fori_loop(0, 8, sum_ac, 0)
+    third = [copy(t.at[(z + k) % 8], rt.at[k - 1], along_z(k)) for k in range(1, 8)]
+    for made in second_b:
+        made.wait()
+
+    def sum_b2(i, carry):
+        total = wide(sb[y, i])
+        for k in range(3):
+            total += wide(rb2[k, i])
+        tb[i] = total.astype(jnp.bfloat16)
+        return carry
+
+    lax.fori_loop(0, 2, sum_b2, 0)
+    third_b = [copy(tb.at[1 - x], rtb, across)]
+    for made in third + third_b:
+        made.wait()
+    total = wide(t[z])
+    for k in range(7):
+        total += wide(rt[k])
+    out_ref[:AC, :] = total
+    out_ref[AC:, :] = wide(tb[x]) + wide(rtb[...])
+
+
+def reduce_rows(rows, slots):
+    def buf(*shape):
+        return pltpu.VMEM((*shape, HALF), jnp.bfloat16)
+
+    a, b, c = SLOTS_A, SLOTS_B, SLOTS_C
+    count = 2 + 1 + 3 + 7 + 3 + 1 + 3 + 7 + 1
+    return pl.pallas_call(
+        reduce_kernel,
+        out_shape=jax.ShapeDtypeStruct((STACKS_DEV, HALF), jnp.float32),
+        in_specs=[VMEM, VMEM],
+        out_specs=VMEM,
+        scratch_shapes=[
+            buf(CB * CAP), pltpu.VMEM((CB, STACKS_DEV), jnp.int32),
+            buf(4, 16, a), buf(8, 8, b), buf(2, 32, c), buf(3, 16, a), buf(7, 8, b), buf(32, c),
+            buf(2, 8, a), buf(4, 2, b), buf(4, 8, c), buf(8, a), buf(3, 2, b), buf(3, 8, c),
+            buf(8, AC), buf(2, b), buf(7, AC), buf(b),
+            pltpu.SemaphoreType.DMA((count,)), pltpu.SemaphoreType.DMA((count,)),
+        ],
+        compiler_params=pltpu.CompilerParams(
+            collective_id=1, has_side_effects=True, vmem_limit_bytes=40 * 2**20
+        ),
+        cost_estimate=pl.CostEstimate(flops=2_000_000_000, bytes_accessed=2**23, transcendentals=0),
+        name="reduce_rows",
+    )(rows, slots)
+
+
 def local(spectra, owner_device, stack_slot):
     blk_devices = lax.axis_size("blk")
     seg = lax.axis_index("seg")
@@ -223,19 +397,18 @@
         gots.append(lax.ppermute(send, "seg", [(0, 1), (1, 0)]))
 
     owner_rows = owner_device[:, 0]
-    owner_hot = (owner_rows[:, None] == lax.iota(jnp.int32, blk_devices)[None, :]).astype(jnp.int32)
-    position = jnp.sum((jnp.cumsum(owner_hot, axis=0) - owner_hot) * owner_hot, axis=1)
-    destination = owner_rows * CAP + position
-    outgoing = place_rows(destination, keeps, gots, blk_devices * CAP)
-    outgoing_slot = (
-        jnp.full((blk_devices * CAP, 1), -1, jnp.int32).at[destination, 0].set(stack_slot)
+    ordered = (owner_rows % 2) * CB + owner_rows // 2
+    hot = ordered[:, None] == lax.iota(jnp.int32, blk_devices)[None, :]
+    count = hot.astype(jnp.int32)
+    position = jnp.sum((jnp.cumsum(count, axis=0) - count) * count, axis=1)
+    place_hot = position[:, None] == lax.iota(jnp.int32, STACKS_DEV)[None, :] % CAP
+    named = jnp.where(place_hot, (stack_slot + 1)[:, None], 0).astype(jnp.bfloat16)
+    slots = lax.dot_general(
+        hot.astype(jnp.bfloat16), named, (((0,), (0,)), ((), ())), preferred_element_type=jnp.float32
     )
-    received = lax.all_to_all(outgoing, "blk", split_axis=0, concat_axis=0, tiled=True)
-    received_slot = lax.all_to_all(outgoing_slot, "blk", split_axis=0, concat_axis=0, tiled=True)
-    one_hot = (lax.iota(jnp.int32, STACKS_DEV)[:, None] == received_slot[:, 0][None, :]).astype(
-        jnp.bfloat16
-    )
-    stacks = jnp.dot(one_hot, received, preferred_element_type=jnp.float32)
+    slots = slots.astype(jnp.int32) - 1
+    outgoing = place_rows(ordered * CAP + position, keeps, gots, blk_devices * CAP)
+    stacks = reduce_rows(outgoing, slots)
     lags = lax.iota(jnp.int32, HALF)
     turned = jnp.roll(stacks[:, ::-1], 1, axis=1)
     stacks = jnp.where(seg == 0, turned, stacks)

time: 245 us -> 190 us (0.78)
  waiting for transfers between devices: 94.7 us -> 12.4 us
  Pallas kernels: 70 us -> 147 us
  starting transfers between devices: 43.9 us -> 10.1 us
  local copies, waits for them, and re-layouts: 27.9 us -> 12.7 us
    all_to_all x2 -> x0, waiting for transfers between devices: 94.7 us -> none  [the longest x1 94.7 us: local(): lax.all_to_all(outgoing, 'blk', split_axis=0, concat_axis=0, tiled=True)]
    pallas_call x0 -> x1, Pallas kernels: none -> 77 us  [reduce_rows(): pl.pallas_call(reduce_kernel, out_shape=jax.ShapeDtypeStruct((STACKS_DEV,...]
    all_to_all x2 -> x0, starting transfers between devices: 33.9 us -> none  [the longest x1 21.1 us: local(): lax.all_to_all(outgoing_slot, 'blk', split_axis=0, concat_axis=0, tiled=T...]
    unnamed x17 -> x18, local copies, waits for them, and re-layouts: 19.4 us -> 5.58 us
    ppermute x2, waiting for transfers between devices: 0.01 us -> 12.4 us  [local(): gots.append(lax.ppermute(send, 'seg', [(0, 1), (1, 0)]))]
  transfers between devices with their start and end apart: 6 -> 4, of which waited for: 1 -> 1; matrix products, arithmetic and copies ran while one was open for 9% -> 4% of each run, Pallas kernels for 27% -> 23%
where the time goes in v2:
time: 190 us; the launch traced here: 189 us
  Pallas kernels  147 us (77%)
  local copies, waits for them, and re-layouts  12.7 us (7%)
  waiting for transfers between devices  12.4 us (7%)
  starting transfers between devices  10.1 us (5%)
  other arithmetic  3.8 us (2%)
  matrix products  2.44 us (1%)
    pallas_call x1, Pallas kernels, reduce_rows(): pl.pallas_call(reduce_kernel, out_shape=jax.ShapeDtypeStruct((STACKS_DEV,...  77 us
    pallas_call x2, Pallas kernels, tile_halves(): pl.pallas_call(functools.partial(tile_kernel, chans), out_shape=(jax.Shap...  43.2 us
    pallas_call x1, Pallas kernels, place_rows(): pl.pallas_call(functools.partial(place_kernel, chunks), out_shape=jax.Sha...  21.7 us
    ppermute x2, waiting for transfers between devices, local(): gots.append(lax.ppermute(send, 'seg', [(0, 1), (1, 0)]))  12.4 us
    ppermute x2, starting transfers between devices, local(): lax.ppermute(whitened[i * chans:(i + 1) * chans], 'blk', ahead)  6.49 us
    unnamed x18, local copies, waits for them, and re-layouts  5.58 us
    pallas_call x1, Pallas kernels, whiten(): pl.pallas_call(whiten_kernel, out_shape=jax.ShapeDtypeStruct((CB, GROUPS...  5.1 us
    reshape x1, local copies, waits for them, and re-layouts, whiten(): spectra.reshape(4, CB, 2 * F)  4.47 us
  transfers between devices with their start and end apart: 4, of which 1 were waited for; matrix products, arithmetic and copies ran while one was open for 4% of the time, Pallas kernels for 23%

profile of v2, /device:TPU:4, one launch (start us, length us, event | category | flops | bytes accessed | tf_op | source)
XLA Modules:
  0.0 188.6 jit_solution(17322439016447142260)
XLA Ops:
  0.0 4.5 %reshape.41.x_ref = bf16[4,64,4096]{2,1,0:T(8,128)(2,1)} reshape(bf16[4,64,2,2048]{3,2,1,0:T(2,128)(2,1)} %param.5) | data formatting | bytes 4194304 | tf_op jit(solution)/shard_map/reshape | solution.py:83
  4.5 1.6 copy-done.1
  6.1 5.1 %whiten.1.o_ref = bf16[64,16384]{1,0:T(8,128)(2,1)S(1)} custom-call(bf16[4,64,4096]{2,1,0:T(8,128)(2,1)S(1)} %copy-done.1), custom_call_target="tpu_custom_call" | custom-call | flops 20000000 | bytes 4194304 | tf_op jit(solution)/shard_map/whiten/pallas_call | solution.py:75
  11.2 1.2 fusion.25
  12.4 0.4 copy-done
  12.8 2.7 %collective-permute-start = (bf16[32,16384]{1,0:T(8,128)(2,1)}, bf16[32,16384]{1,0:T(8,128)(2,1)}, u32[]{:S(2)}, u32[]{:S(2)}) collective-permute-start(bf16[32,16384]{1,0:T(8,128)(2,1)} %get-tuple-element.14), channel_id=1, source_target_pairs={{0,2},{2,4},{4,6},{6,8},{8,10},{10,12},{12,14},{14,16},{16,18},{18... | collective-permute-start | bytes 3145736 | tf_op jit(solution)/shard_map/ppermute | solution.py:390
  15.6 3.8 %collective-permute-start.1 = (bf16[32,16384]{1,0:T(8,128)(2,1)S(1)}, bf16[32,16384]{1,0:T(8,128)(2,1)}, u32[]{:S(2)}, u32[]{:S(2)}) collective-permute-start(bf16[32,16384]{1,0:T(8,128)(2,1)S(1)} %get-tuple-element.13), channel_id=1, source_target_pairs={{0,2},{2,4},{4,6},{6,8},{8,10},{10,12},{12,14},{14,16},{16,18},{18... | collective-permute-start | bytes 3145736 | tf_op jit(solution)/shard_map/ppermute | solution.py:390
  19.6 0.6 fusion.2
  20.3 21.6 %tiles.2 = (f32[256,2048]{1,0:T(8,128)}, bf16[256,2048]{1,0:T(8,128)(2,1)}) custom-call(s32[1]{0:T(128)} %bitcast.6.sign_ref, bf16[32,16384]{1,0:T(8,128)(2,1)} %collective-permute-done.p_ref, bf16[64,16384]{1,0:T(8,128)(2,1)} %copy-done, bf16[272,2048]{1,0:T(8,128)(2,1)} %constant.62.clone.cos_ref, bf16[256,2048]{1,0:T(8,128)(2,1)} %constant.63.clone.sin_ref), custom_call_target="tpu_custom_call" | custom-call | flops 12499999744 | bytes 8388608 | tf_op jit(solution)/shard_map/tiles/pallas_call | solution.py:140
  41.8 0.6 collective-permute-start.2
  42.4 21.6 %tiles.3 = (f32[256,2048]{1,0:T(8,128)}, bf16[256,2048]{1,0:T(8,128)(2,1)}) custom-call(s32[1]{0:T(128)} %bitcast.6.sign_ref, bf16[32,16384]{1,0:T(8,128)(2,1)} %collective-permute-done.1.p_ref, bf16[64,16384]{1,0:T(8,128)(2,1)} %copy-done, bf16[272,2048]{1,0:T(8,128)(2,1)} %constant.62.clone.cos_ref, bf16[256,2048]{1,0:T(8,128)(2,1)} %constant.63.clone.sin_ref), custom_call_target="tpu_custom_call" | custom-call | flops 12499999744 | bytes 8388608 | tf_op jit(solution)/shard_map/tiles/pallas_call | solution.py:140
  64.0 3.0 %collective-permute-start.3 = (bf16[256,2048]{1,0:T(8,128)(2,1)}, bf16[256,2048]{1,0:T(8,128)(2,1)S(1)}, u32[]{:S(2)}, u32[]{:S(2)}) collective-permute-start(bf16[256,2048]{1,0:T(8,128)(2,1)} %get-tuple-element.12), channel_id=1, source_target_pairs={{0,1},{1,0},{2,3},{3,2},{4,5},{5,4},{6,7},{7,6},{8,9},{9,8},{10,11... | collective-permute-start | bytes 3145736 | tf_op jit(solution)/shard_map/ppermute | solution.py:397
  67.0 0.2 broadcast_add_fusion
  67.3 1.2 copy.8
  68.5 1.4 fusion.1
  70.0 0.6 fusion.17.dest_ref
  70.6 2.4 %fusion.6.slots_ref = s32[128,128]{1,0:T(8,128)S(1)} fusion(s32[4096]{0:T(1024)S(1)} %broadcast_add_fusion.1, s32[128]{0:T(128)S(1)} %and_select_fusion.2, s32[4096]{0:T(1024)S(1)} %bitcast.18, s32[4096]{0:T(1024)S(1)} %fusion.1), kind=kOutput, calls=%fused_computation.10 | convolution fusion | flops 136347648 | bytes 115200 | tf_op jit(solution)/shard_map/dot_general | solution.py:406
  73.1 12.4 %collective-permute-done.3.refs_3_ = bf16[256,2048]{1,0:T(8,128)(2,1)S(1)} collective-permute-done((bf16[256,2048]{1,0:T(8,128)(2,1)}, bf16[256,2048]{1,0:T(8,128)(2,1)S(1)}, u32[]{:S(2)}, u32[]{:S(2)}) %collective-permute-start.3) | collective-permute-done | bytes 1048608 | tf_op jit(solution)/shard_map/ppermute | solution.py:397
  85.5 1.1 copy-done.4
  86.5 21.7 %place.1.rows_ref = bf16[8192,256]{1,0:T(8,128)(2,1)} custom-call(s32[4096]{0:T(1024)} %fusion.17.dest_ref, f32[256,2048]{1,0:T(8,128)} %get-tuple-element.9.refs_0_, f32[256,2048]{1,0:T(8,128)} %get-tuple-element.10.refs_1_, bf16[256,2048]{1,0:T(8,128)(2,1)} %copy-done.3, bf16[256,2048]{1,0:T(8,128)(2,1)} %copy-done.4), custom_call_target="tpu_custom_call" | custom-call | tf_op jit(solution)/shard_map/place/pallas_call | solution.py:192
  108.2 2.2 %copy-done.2 = bf16[8192,256]{1,0:T(8,128)(2,1)S(1)} copy-done((bf16[8192,256]{1,0:T(8,128)(2,1)S(1)}, bf16[8192,256]{1,0:T(8,128)(2,1)}, u32[]{:S(2)}) %copy-start.2) | copy-done | bytes 4194328
  110.4 77.0 %reduce_rows.1 = f32[128,256]{1,0:T(8,128)S(1)} custom-call(bf16[8192,256]{1,0:T(8,128)(2,1)S(1)} %copy-done.2, s32[128,128]{1,0:T(8,128)S(1)} %fusion.6.slots_ref), custom_call_target="tpu_custom_call" | custom-call | flops 2000000000 | bytes 8388608 | tf_op jit(solution)/shard_map/reduce_rows/pallas_call | solution.py:360
  187.5 0.2 reverse.2
  187.8 0.7 fusion.13
  (26 shorter events, 0.5 us)
Async XLA Ops:
  4.5 1.6 copy-start.1
  11.2 1.7 copy-start
  11.2 8.1 %copy-start.6 = (s32[4096,1]{0,1:T(1,128)S(1)}, s32[4096,1]{0,1:T(1,128)}, u32[]{:S(2)}) copy-start(s32[4096,1]{0,1:T(1,128)} %param.6) | copy-start | bytes 49156
  12.8 7.4 %collective-permute-start = (bf16[32,16384]{1,0:T(8,128)(2,1)}, bf16[32,16384]{1,0:T(8,128)(2,1)}, u32[]{:S(2)}, u32[]{:S(2)}) collective-permute-start(bf16[32,16384]{1,0:T(8,128)(2,1)} %get-tuple-element.14), channel_id=1, source_target_pairs={{0,2},{2,4},{4,6},{6,8},{8,10},{10,12},{12,14},{14,16},{16,18},{18... | collective-permute-start | bytes 3145736 | tf_op jit(solution)/shard_map/ppermute | solution.py:390
  15.6 26.9 %collective-permute-start.1 = (bf16[32,16384]{1,0:T(8,128)(2,1)S(1)}, bf16[32,16384]{1,0:T(8,128)(2,1)}, u32[]{:S(2)}, u32[]{:S(2)}) collective-permute-start(bf16[32,16384]{1,0:T(8,128)(2,1)S(1)} %get-tuple-element.13), channel_id=1, source_target_pairs={{0,2},{2,4},{4,6},{6,8},{8,10},{10,12},{12,14},{14,16},{16,18},{18... | collective-permute-start | bytes 3145736 | tf_op jit(solution)/shard_map/ppermute | solution.py:390
  20.2 21.6 %copy-start.5 = (s32[128,33]{0,1:T(8,128)}, s32[128,33]{0,1:T(8,128)S(1)}, u32[]{:S(2)}) copy-start(s32[128,33]{0,1:T(8,128)S(1)} %reduce-window.9) | copy-start | bytes 50692
  41.8 25.2 %slice-start = ((s32[128,33]{0,1:T(8,128)}), s32[128,32]{0,1:T(8,128)S(1)}, s32[]{:S(2)}) async-start(s32[128,33]{0,1:T(8,128)} %copy-done.5), calls=%async_computation | async-start | bytes 32768 | tf_op jit(solution)/shard_map/slice.3
  41.8 31.2 %collective-permute-start.2 = (bf16[256,2048]{1,0:T(8,128)(2,1)}, bf16[256,2048]{1,0:T(8,128)(2,1)S(1)}, u32[]{:S(2)}, u32[]{:S(2)}) collective-permute-start(bf16[256,2048]{1,0:T(8,128)(2,1)} %get-tuple-element.11), channel_id=1, source_target_pairs={{0,1},{1,0},{2,3},{3,2},{4,5},{5,4},{6,7},{7,6},{8,9},{9,8},{10,11... | collective-permute-start | bytes 3145736 | tf_op jit(solution)/shard_map/ppermute | solution.py:397
  64.0 21.4 %collective-permute-start.3 = (bf16[256,2048]{1,0:T(8,128)(2,1)}, bf16[256,2048]{1,0:T(8,128)(2,1)S(1)}, u32[]{:S(2)}, u32[]{:S(2)}) collective-permute-start(bf16[256,2048]{1,0:T(8,128)(2,1)} %get-tuple-element.12), channel_id=1, source_target_pairs={{0,1},{1,0},{2,3},{3,2},{4,5},{5,4},{6,7},{7,6},{8,9},{9,8},{10,11... | collective-permute-start | bytes 3145736 | tf_op jit(solution)/shard_map/ppermute | solution.py:397
  67.3 1.2 copy-start.7
  73.1 12.4 %copy-start.3 = (bf16[256,2048]{1,0:T(8,128)(2,1)}, bf16[256,2048]{1,0:T(8,128)(2,1)S(1)}, u32[]{:S(2)}) copy-start(bf16[256,2048]{1,0:T(8,128)(2,1)S(1)} %collective-permute-done.2.refs_2_) | copy-start | bytes 3145732
  85.4 1.1 copy-start.4
  108.2 2.2 %copy-start.2 = (bf16[8192,256]{1,0:T(8,128)(2,1)S(1)}, bf16[8192,256]{1,0:T(8,128)(2,1)}, u32[]{:S(2)}) copy-start(bf16[8192,256]{1,0:T(8,128)(2,1)} %place.1.rows_ref) | copy-start | bytes 12582916

commit v3 on v2

--- a/solution.py
+++ b/solution.py
@@ -84,37 +84,31 @@
 
 
 def tile_kernel(chans, sign_ref, p_ref, o_ref, cos_ref, sin_ref, keep_ref, send_ref, g_re, g_im):
-    unroll = 4
+    unroll = 32
     row = lax.broadcasted_iota(jnp.int32, (GROUP, WIDE), 0)
     lane = lax.broadcasted_iota(jnp.int32, (GROUP, WIDE), 1)
     mask = jnp.where(row == lane % GROUP, 1.0, 0.0).astype(jnp.bfloat16)
     wide_lane = lax.broadcasted_iota(jnp.int32, (CB, WIDE), 1)
     turn = jnp.where(wide_lane < WIDE // 2, -1.0, 1.0).astype(jnp.bfloat16)
-    zero = jnp.zeros((CB, WIDE), jnp.bfloat16)
 
     def one(group):
         cols = pl.ds(pl.multiple_of(group * WIDE, WIDE), WIDE)
         own = o_ref[:, cols]
-        turned = jnp.concatenate([own[:, WIDE // 2 :], own[:, : WIDE // 2]], axis=1) * turn
-        right = jnp.concatenate(
-            [
-                jnp.concatenate([own, zero], 1),
-                jnp.concatenate([zero, own], 1),
-                jnp.concatenate([turned, zero], 1),
-                jnp.concatenate([zero, turned], 1),
-            ],
-            0,
-        )
+        turned = jnp.concatenate([own[:, CB:], own[:, :CB]], axis=1) * turn
         spread = jnp.broadcast_to(p_ref[:, cols][:, None, :], (chans, GROUP, WIDE)) * mask[None]
-        spread = spread.reshape(chans // 2, 2, GROUP, WIDE)
-        left = jnp.concatenate([spread[:, 0], spread[:, 1]], axis=2).reshape(chans * 8, 2 * WIDE)
         out = lax.dot_general(
-            left, right, (((1,), (1,)), ((), ())), preferred_element_type=jnp.float32
+            spread.reshape(chans * GROUP, WIDE),
+            jnp.concatenate([own, turned], 0),
+            (((1,), (1,)), ((), ())),
+            preferred_element_type=jnp.float32,
         ).astype(jnp.bfloat16)
         rows = pl.ds(pl.multiple_of(group * GROUP, GROUP), GROUP)
         for i in range(chans // 2):
-            g_re[rows, i * WIDE : (i + 1) * WIDE] = out[i * GROUP : (i + 1) * GROUP, :WIDE]
-            g_im[rows, i * WIDE : (i + 1) * WIDE] = out[i * GROUP : (i + 1) * GROUP, WIDE:]
+            first = out[2 * i * GROUP : (2 * i + 1) * GROUP]
+            second = out[(2 * i + 1) * GROUP : (2 * i + 2) * GROUP]
+            pair = slice(i * WIDE, (i + 1) * WIDE)
+            g_re[rows, pair] = jnp.concatenate([first[:, :CB], second[:, :CB]], 1)
+            g_im[rows, pair] = jnp.concatenate([first[:, CB:], second[:, CB:]], 1)
 
     def body(i, carry):
         for u in range(unroll):
@@ -146,7 +140,7 @@
         in_specs=[SMEM, VMEM, VMEM, VMEM, VMEM],
         out_specs=(VMEM, VMEM),
         scratch_shapes=[pltpu.VMEM((F, pairs), jnp.bfloat16)] * 2,
-        compiler_params=pltpu.CompilerParams(vmem_limit_bytes=56 * 2**20),
+        compiler_params=pltpu.CompilerParams(vmem_limit_bytes=24 * 2**20),
         cost_estimate=pl.CostEstimate(
             flops=25_000_000_000 * chans // CB, bytes_accessed=2**23, transcendentals=0
         ),
@@ -162,43 +156,46 @@
         for j in range(pairs // 256):
             cols = slice(j * 256, (j + 1) * 256)
             total = keeps[chunk][:, cols] + gots[chunk][:, cols].astype(jnp.float32)
-            first = chunk * pairs + j * 256
-            rows[first : first + 256, :] = total.T
+            turned = total.T
+            for side in range(2):
+                at = pl.ds((chunk * pairs + j * 256) * 2 + side, 256, stride=2)
+                rows[at, :] = turned[:, side * WIDE : (side + 1) * WIDE]
 
     def clear(i, carry):
-        spread[pl.ds(pl.multiple_of(i * 64, 64), 64), :] = jnp.zeros((64, HALF), jnp.float32)
-        return carry
-
-    lax.fori_loop(0, spread.shape[0] // 64, clear, 0)
+        spread[pl.ds(pl.multiple_of(i * 512, 512), 512), :] = jnp.zeros((512, WIDE), jnp.float32)
+        return carry
+
+    lax.fori_loop(0, spread.shape[0] // 512, clear, 0)
 
     def move(i, carry):
-        for u in range(16):
-            p = i * 16 + u
-            spread[pl.ds(dest_ref[p], 1), :] = rows[pl.ds(p, 1), :]
-        return carry
-
-    lax.fori_loop(0, PAIRS // 16, move, 0)
+        for u in range(64):
+            p = i * 64 + u
+            to = pl.multiple_of(dest_ref[p] * 2, 2)
+            spread[pl.ds(to, 2), :] = rows[pl.ds(pl.multiple_of(p * 2, 2), 2), :]
+        return carry
+
+    lax.fori_loop(0, PAIRS // 64, move, 0)
 
     def finish(i, carry):
-        at = pl.ds(pl.multiple_of(i * 64, 64), 64)
+        at = pl.ds(pl.multiple_of(i * 512, 512), 512)
         out_ref[at, :] = spread[at, :].astype(jnp.bfloat16)
         return carry
 
-    lax.fori_loop(0, spread.shape[0] // 64, finish, 0)
+    lax.fori_loop(0, spread.shape[0] // 512, finish, 0)
 
 
 def place_rows(dest, keeps, gots, rows_out):
     chunks = len(keeps)
     return pl.pallas_call(
         functools.partial(place_kernel, chunks),
-        out_shape=jax.ShapeDtypeStruct((rows_out, HALF), jnp.bfloat16),
+        out_shape=jax.ShapeDtypeStruct((2 * rows_out, WIDE), jnp.bfloat16),
         in_specs=[SMEM] + [VMEM] * (2 * chunks),
         out_specs=VMEM,
         scratch_shapes=[
-            pltpu.VMEM((PAIRS, HALF), jnp.float32),
-            pltpu.VMEM((rows_out, HALF), jnp.float32),
+            pltpu.VMEM((2 * PAIRS, WIDE), jnp.float32),
+            pltpu.VMEM((2 * rows_out, WIDE), jnp.float32),
         ],
-        compiler_params=pltpu.CompilerParams(vmem_limit_bytes=56 * 2**20),
+        compiler_params=pltpu.CompilerParams(vmem_limit_bytes=28 * 2**20),
         name="place",
     )(dest, *keeps, *gots)
 
@@ -248,33 +245,41 @@
         made.start()
         return made
 
-    half = CB * CAP
+    half = 2 * CB * CAP
     copies = [
         copy(rows_ref.at[pl.ds((1 - core) * half, half)], sib_rows, other),
         copy(slots_ref.at[pl.ds((1 - core) * CB, CB)], sib_slots, other),
     ]
     for made in copies:
         made.wait()
-    lane = lax.broadcasted_iota(jnp.int32, (1, STACKS_DEV), 1)
-    slot = lax.broadcasted_iota(jnp.int32, (STACKS_DEV, STACKS_DEV), 0)
-
-    def dense(i, carry):
+    lane = lax.broadcasted_iota(jnp.int32, (1, 4 * CAP), 1)
+    slot = lax.broadcasted_iota(jnp.int32, (STACKS_DEV, 4 * CAP), 0)
+    span = 2 * CAP
+
+    def dense_one(i):
         zz, xx, yy = i // 8, (i // 4) % 2, i % 4
-        names = jnp.where(
-            lane < CAP, slots_ref[pl.ds(core * CB + i, 1), :], sib_slots[pl.ds(i, 1), :]
-        )
-        hot = jnp.where(slot == names, 1.0, 0.0).astype(jnp.bfloat16)
-        mine = rows_ref[pl.ds(pl.multiple_of(core * half + i * CAP, CAP), CAP), :]
-        theirs = sib_rows[pl.ds(pl.multiple_of(i * CAP, CAP), CAP), :]
+        names = jnp.concatenate([slots_ref[pl.ds(core * CB + i, 1), :], sib_slots[pl.ds(i, 1), :]], 1)
+        left = jnp.where(lane % 2 == 0, names, -1)
+        right = jnp.where(lane % 2 == 1, names, -1)
+        hot = jnp.concatenate([slot == left, slot == right], 0)
+        mine = rows_ref[pl.ds(pl.multiple_of(core * half + i * span, span), span), :]
+        theirs = sib_rows[pl.ds(pl.multiple_of(i * span, span), span), :]
         total = jnp.dot(
-            hot, jnp.concatenate([mine, theirs], 0), preferred_element_type=jnp.float32
+            jnp.where(hot, 1.0, 0.0).astype(jnp.bfloat16),
+            jnp.concatenate([mine, theirs], 0),
+            preferred_element_type=jnp.float32,
         ).astype(jnp.bfloat16)
+        total = jnp.concatenate([total[:STACKS_DEV], total[STACKS_DEV:]], 1)
         da[yy, zz * 2 + xx] = total[:SLOTS_A]
         dc[xx, zz * 4 + yy] = total[SLOTS_A:AC]
         db[zz, xx * 4 + yy] = total[AC:]
-        return carry
-
-    lax.fori_loop(0, CB, dense, 0)
+
+    def dense(i, carry):
+        for u in range(8):
+            dense_one(i * 8 + u)
+        return carry
+
+    lax.fori_loop(0, CB // 8, dense, 0)
     first_c = [copy(dc.at[1 - x], rc, across)]
     first_a = [copy(da.at[(y + k) % 4], ra.at[k - 1], along_y(k)) for k in (1, 2, 3)]
     first_b = [copy(db.at[(z + k) % 8], rb.at[k - 1], along_z(k)) for k in range(1, 8)]
@@ -363,7 +368,7 @@
         in_specs=[VMEM, VMEM],
         out_specs=VMEM,
         scratch_shapes=[
-            buf(CB * CAP), pltpu.VMEM((CB, STACKS_DEV), jnp.int32),
+            pltpu.VMEM((2 * CB * CAP, WIDE), jnp.bfloat16), pltpu.VMEM((CB, STACKS_DEV), jnp.int32),
             buf(4, 16, a), buf(8, 8, b), buf(2, 32, c), buf(3, 16, a), buf(7, 8, b), buf(32, c),
             buf(2, 8, a), buf(4, 2, b), buf(4, 8, c), buf(8, a), buf(3, 2, b), buf(3, 8, c),
             buf(8, AC), buf(2, b), buf(7, AC), buf(b),
@@ -382,7 +387,7 @@
     seg = lax.axis_index("seg")
     factor = (2.0 * F * SEGS) ** (-0.5)
     cos_rows, sin_rows = lag_rows(factor)
-    chunks = 2
+    chunks = 4
     chans = CB // chunks
     whitened = whiten(spectra)
     ahead = [(b, b + 1) for b in range(blk_devices - 1)]
@@ -401,7 +406,7 @@
     hot = ordered[:, None] == lax.iota(jnp.int32, blk_devices)[None, :]
     count = hot.astype(jnp.int32)
     position = jnp.sum((jnp.cumsum(count, axis=0) - count) * count, axis=1)
-    place_hot = position[:, None] == lax.iota(jnp.int32, STACKS_DEV)[None, :] % CAP
+    place_hot = position[:, None] == lax.iota(jnp.int32, STACKS_DEV)[None, :] // 2
     named = jnp.where(place_hot, (stack_slot + 1)[:, None], 0).astype(jnp.bfloat16)
     slots = lax.dot_general(
         hot.astype(jnp.bfloat16), named, (((0,), (0,)), ((), ())), preferred_element_type=jnp.float32

time: 190 us -> 159 us (0.84)
  Pallas kernels: 147 us -> 97.8 us
  starting transfers between devices: 10.1 us -> 18.9 us
  waiting for transfers between devices: 12.4 us -> 18.4 us
  other arithmetic: 3.8 us -> 7.34 us
    pallas_call x1, Pallas kernels: 77 us -> 56.7 us  [reduce_rows(): pl.pallas_call(reduce_kernel, out_shape=jax.ShapeDtypeStruct((STACKS_DEV,...]
    pallas_call x2 -> x4, Pallas kernels: 43.2 us -> 28.2 us  [tile_halves(): pl.pallas_call(functools.partial(tile_kernel, chans), out_shape=(jax.Shap...]
    pallas_call x1, Pallas kernels: 21.7 us -> 7.74 us  [place_rows(): pl.pallas_call(functools.partial(place_kernel, chunks), out_shape=jax.Sha...]
    ppermute x2 -> x4, waiting for transfers between devices: 12.4 us -> 18.4 us  [local(): gots.append(lax.ppermute(send, 'seg', [(0, 1), (1, 0)]))]
    ppermute x2 -> x4, starting transfers between devices: 6.49 us -> 11 us  [local(): lax.ppermute(whitened[i * chans:(i + 1) * chans], 'blk', ahead)]
    ppermute x2 -> x4, starting transfers between devices: 3.59 us -> 7.81 us  [local(): gots.append(lax.ppermute(send, 'seg', [(0, 1), (1, 0)]))]
    another operation x3, other arithmetic: 0.89 us -> 3.82 us
    another operation x4 -> x3, local copies, waits for them, and re-layouts: 1.23 us -> 4.15 us
  transfers between devices with their start and end apart: 4 -> 8, of which waited for: 1 -> 2; matrix products, arithmetic and copies ran while one was open for 4% -> 8% of each run, Pallas kernels for 23% -> 18%
where the time goes in v3:
time: 159 us; the launch traced here: 158 us
  Pallas kernels  97.8 us (62%)
  starting transfers between devices  18.9 us (12%)
  waiting for transfers between devices  18.4 us (12%)
  local copies, waits for them, and re-layouts  13.4 us (8%)
  other arithmetic  7.34 us (5%)
  matrix products  2.44 us (2%)
    pallas_call x1, Pallas kernels, reduce_rows(): pl.pallas_call(reduce_kernel, out_shape=jax.ShapeDtypeStruct((STACKS_DEV,...  56.7 us
    pallas_call x4, Pallas kernels, tile_halves(): pl.pallas_call(functools.partial(tile_kernel, chans), out_shape=(jax.Shap...  28.2 us
    ppermute x4, waiting for transfers between devices, local(): gots.append(lax.ppermute(send, 'seg', [(0, 1), (1, 0)]))  18.4 us
    ppermute x4, starting transfers between devices, local(): lax.ppermute(whitened[i * chans:(i + 1) * chans], 'blk', ahead)  11 us
    ppermute x4, starting transfers between devices, local(): gots.append(lax.ppermute(send, 'seg', [(0, 1), (1, 0)]))  7.81 us
    pallas_call x1, Pallas kernels, place_rows(): pl.pallas_call(functools.partial(place_kernel, chunks), out_shape=jax.Sha...  7.74 us
    pallas_call x1, Pallas kernels, whiten(): pl.pallas_call(whiten_kernel, out_shape=jax.ShapeDtypeStruct((CB, GROUPS...  5.1 us
    reshape x1, local copies, waits for them, and re-layouts, whiten(): spectra.reshape(4, CB, 2 * F)  4.47 us
  transfers between devices with their start and end apart: 8, of which 2 were waited for; matrix products, arithmetic and copies ran while one was open for 8% of the time, Pallas kernels for 18%

profile of v3, /device:TPU:4, one launch (start us, length us, event | category | flops | bytes accessed | tf_op | source)
XLA Modules:
  0.0 158.4 jit_solution(9882518676865626363)
XLA Ops:
  0.0 4.5 %reshape.63.x_ref = bf16[4,64,4096]{2,1,0:T(8,128)(2,1)} reshape(bf16[4,64,2,2048]{3,2,1,0:T(2,128)(2,1)} %param.5) | data formatting | bytes 4194304 | tf_op jit(solution)/shard_map/reshape | solution.py:83
  4.5 1.6 %copy-done = bf16[4,64,4096]{2,1,0:T(8,128)(2,1)S(1)} copy-done((bf16[4,64,4096]{2,1,0:T(8,128)(2,1)S(1)}, bf16[4,64,4096]{2,1,0:T(8,128)(2,1)}, u32[]{:S(2)}) %copy-start) | copy-done | bytes 2097176
  6.1 5.1 %whiten.1.o_ref = bf16[64,16384]{1,0:T(8,128)(2,1)S(1)} custom-call(bf16[4,64,4096]{2,1,0:T(8,128)(2,1)S(1)} %copy-done), custom_call_target="tpu_custom_call" | custom-call | flops 20000000 | bytes 4194304 | tf_op jit(solution)/shard_map/whiten/pallas_call | solution.py:75
  11.2 1.4 fusion.25
  12.5 2.5 %collective-permute-start = (bf16[16,16384]{1,0:T(8,128)(2,1)}, bf16[16,16384]{1,0:T(8,128)(2,1)}, u32[]{:S(2)}, u32[]{:S(2)}) collective-permute-start(bf16[16,16384]{1,0:T(8,128)(2,1)} %get-tuple-element.24), channel_id=1, source_target_pairs={{0,2},{2,4},{4,6},{6,8},{8,10},{10,12},{12,14},{14,16},{16,18},{18... | collective-permute-start | bytes 1572872 | tf_op jit(solution)/shard_map/ppermute | solution.py:395
  15.1 3.8 %collective-permute-start.1 = (bf16[16,16384]{1,0:T(8,128)(2,1)}, bf16[16,16384]{1,0:T(8,128)(2,1)}, u32[]{:S(2)}, u32[]{:S(2)}) collective-permute-start(bf16[16,16384]{1,0:T(8,128)(2,1)} %get-tuple-element.23), channel_id=1, source_target_pairs={{0,2},{2,4},{4,6},{6,8},{8,10},{10,12},{12,14},{14,16},{16,18},{18... | collective-permute-start | bytes 1572872 | tf_op jit(solution)/shard_map/ppermute | solution.py:395
  18.9 1.3 collective-permute-start.2
  20.2 3.4 %collective-permute-start.3 = (bf16[16,16384]{1,0:T(8,128)(2,1)}, bf16[16,16384]{1,0:T(8,128)(2,1)S(1)}, u32[]{:S(2)}, u32[]{:S(2)}) collective-permute-start(bf16[16,16384]{1,0:T(8,128)(2,1)} %get-tuple-element.21), channel_id=1, source_target_pairs={{0,2},{2,4},{4,6},{6,8},{8,10},{10,12},{12,14},{14,16},{16,18},{18... | collective-permute-start | bytes 1572872 | tf_op jit(solution)/shard_map/ppermute | solution.py:395
  24.5 1.3 copy-done.3
  25.9 3.1 %broadcast_add_fusion = s32[128,32,128]{0,1,2:T(8,128)} fusion(s32[128,32,128]{0,1,2:T(8,128)} %copy-done.3, s32[128,32]{0,1:T(8,128)S(1)} %slice.40), kind=kLoop, calls=%fused_computation.14 | loop fusion | flops 524288 | bytes 4210688 | tf_op jit(solution)/shard_map/reduce_window_sum
  29.0 4.1 %copy.8 = s32[128,32,128]{0,2,1:T(8,128)} copy(s32[128,32,128]{0,1,2:T(8,128)} %broadcast_add_fusion) | data formatting | bytes 4194304 | tf_op jit(solution)/shard_map/reduce_window_sum
  33.2 2.7 %fusion.1 = s32[4096]{0:T(1024)S(1)} fusion(s32[128,32,128]{0,2,1:T(8,128)} %copy.8, s32[4096]{0:T(1024)S(1)} %bitcast.17), kind=kLoop, calls=%fused_computation.2 | loop fusion | flops 2617344 | bytes 2129920 | tf_op jit(solution)/shard_map/reduce_sum | solution.py:408
  35.9 7.6 %tiles.4 = (f32[256,1024]{1,0:T(8,128)S(1)}, bf16[256,1024]{1,0:T(8,128)(2,1)S(1)}) custom-call(s32[1]{0:T(128)} %bitcast.6.sign_ref, bf16[16,16384]{1,0:T(8,128)(2,1)} %collective-permute-done.p_ref, bf16[64,16384]{1,0:T(8,128)(2,1)S(1)} %whiten.1.o_ref, bf16[272,2048]{1,0:T(8,128)(2,1)S(1)} %copy-done.1, bf16[256,2048]{1,0:T(8,128)(2,1)S(1)} %copy-done.2), custom_call_target="tpu_custom_call" | custom-call | flops 6249999872 | bytes 8388608 | tf_op jit(solution)/shard_map/tiles/pallas_call | solution.py:134
  43.4 0.8 collective-permute-start.4
  44.2 7.6 %tiles.5 = (f32[256,1024]{1,0:T(8,128)S(1)}, bf16[256,1024]{1,0:T(8,128)(2,1)S(1)}) custom-call(s32[1]{0:T(128)} %bitcast.6.sign_ref, bf16[16,16384]{1,0:T(8,128)(2,1)} %collective-permute-done.1.p_ref, bf16[64,16384]{1,0:T(8,128)(2,1)S(1)} %whiten.1.o_ref, bf16[272,2048]{1,0:T(8,128)(2,1)S(1)} %copy-done.1, bf16[256,2048]{1,0:T(8,128)(2,1)S(1)} %copy-done.2), custom_call_target="tpu_custom_call" | custom-call | flops 6249999872 | bytes 8388608 | tf_op jit(solution)/shard_map/tiles/pallas_call | solution.py:134
  51.8 3.1 %collective-permute-start.5 = (bf16[256,1024]{1,0:T(8,128)(2,1)S(1)}, bf16[256,1024]{1,0:T(8,128)(2,1)S(1)}, u32[]{:S(2)}, u32[]{:S(2)}) collective-permute-start(bf16[256,1024]{1,0:T(8,128)(2,1)S(1)} %get-tuple-element.18), channel_id=1, source_target_pairs={{0,1},{1,0},{2,3},{3,2},{4,5},{5,4},{6,7},{7,6},{8,9},{9,8},{10,11... | collective-permute-start | bytes 1572872 | tf_op jit(solution)/shard_map/ppermute | solution.py:402
  54.9 6.5 %tiles.6 = (f32[256,1024]{1,0:T(8,128)S(1)}, bf16[256,1024]{1,0:T(8,128)(2,1)S(1)}) custom-call(s32[1]{0:T(128)} %bitcast.6.sign_ref, bf16[16,16384]{1,0:T(8,128)(2,1)S(1)} %collective-permute-done.2.p_ref, bf16[64,16384]{1,0:T(8,128)(2,1)S(1)} %whiten.1.o_ref, bf16[272,2048]{1,0:T(8,128)(2,1)S(1)} %copy-done.1, bf16[256,2048]{1,0:T(8,128)(2,1)S(1)} %copy-done.2), custom_call_target="tpu_custom_call" | custom-call | flops 6249999872 | bytes 8388608 | tf_op jit(solution)/shard_map/tiles/pallas_call | solution.py:134
  62.0 6.5 %tiles.7 = (f32[256,1024]{1,0:T(8,128)S(1)}, bf16[256,1024]{1,0:T(8,128)(2,1)S(1)}) custom-call(s32[1]{0:T(128)} %bitcast.6.sign_ref, bf16[16,16384]{1,0:T(8,128)(2,1)S(1)} %collective-permute-done.3.p_ref, bf16[64,16384]{1,0:T(8,128)(2,1)S(1)} %whiten.1.o_ref, bf16[272,2048]{1,0:T(8,128)(2,1)S(1)} %copy-done.1, bf16[256,2048]{1,0:T(8,128)(2,1)S(1)} %copy-done.2), custom_call_target="tpu_custom_call" | custom-call | flops 6249999872 | bytes 8388608 | tf_op jit(solution)/shard_map/tiles/pallas_call | solution.py:134
  68.5 3.3 %collective-permute-start.7 = (bf16[256,1024]{1,0:T(8,128)(2,1)S(1)}, bf16[256,1024]{1,0:T(8,128)(2,1)S(1)}, u32[]{:S(2)}, u32[]{:S(2)}) collective-permute-start(bf16[256,1024]{1,0:T(8,128)(2,1)S(1)} %get-tuple-element.20), channel_id=1, source_target_pairs={{0,1},{1,0},{2,3},{3,2},{4,5},{5,4},{6,7},{7,6},{8,9},{9,8},{10,11... | collective-permute-start | bytes 1572872 | tf_op jit(solution)/shard_map/ppermute | solution.py:402
  71.9 2.4 %fusion.6.slots_ref = s32[128,128]{1,0:T(8,128)S(1)} fusion(s32[4096]{0:T(1024)S(1)} %broadcast_add_fusion.1, s32[128]{0:T(128)S(1)} %and_select_fusion.2, s32[4096]{0:T(1024)S(1)} %bitcast.18, s32[4096]{0:T(1024)S(1)} %fusion.1), kind=kOutput, calls=%fused_computation.10 | convolution fusion | flops 136347648 | bytes 115200 | tf_op jit(solution)/shard_map/dot_general | solution.py:411
  74.4 8.1 %collective-permute-done.6.refs_6_ = bf16[256,1024]{1,0:T(8,128)(2,1)S(1)} collective-permute-done((bf16[256,1024]{1,0:T(8,128)(2,1)S(1)}, bf16[256,1024]{1,0:T(8,128)(2,1)S(1)}, u32[]{:S(2)}, u32[]{:S(2)}) %collective-permute-start.6) | collective-permute-done | bytes 524320 | tf_op jit(solution)/shard_map/ppermute | solution.py:402
  82.5 10.3 %collective-permute-done.7.refs_7_ = bf16[256,1024]{1,0:T(8,128)(2,1)S(1)} collective-permute-done((bf16[256,1024]{1,0:T(8,128)(2,1)S(1)}, bf16[256,1024]{1,0:T(8,128)(2,1)S(1)}, u32[]{:S(2)}, u32[]{:S(2)}) %collective-permute-start.7) | collective-permute-done | bytes 524320 | tf_op jit(solution)/shard_map/ppermute | solution.py:402
  92.7 7.7 %place.1.rows_ref = bf16[16384,128]{1,0:T(8,128)(2,1)S(1)} custom-call(s32[4096]{0:T(1024)S(1)} %fusion.17.dest_ref, f32[256,1024]{1,0:T(8,128)S(1)} %get-tuple-element.13.refs_0_, f32[256,1024]{1,0:T(8,128)S(1)} %get-tuple-element.14.refs_1_, f32[256,1024]{1,0:T(8,128)S(1)} %get-tuple-element.15.refs_2_, f32[256,1024]{1,0:T(8,128)S(1)} %get-tuple-element.16.refs_3_, ...), custom_call_target="tpu_custom_call" | custom-call | tf_op jit(solution)/shard_map/place/pallas_call | solution.py:189
  100.4 56.7 %reduce_rows.1 = f32[128,256]{1,0:T(8,128)S(1)} custom-call(bf16[16384,128]{1,0:T(8,128)(2,1)S(1)} %place.1.rows_ref, s32[128,128]{1,0:T(8,128)S(1)} %fusion.6.slots_ref), custom_call_target="tpu_custom_call" | custom-call | flops 2000000000 | bytes 8388608 | tf_op jit(solution)/shard_map/reduce_rows/pallas_call | solution.py:365
  (31 shorter events, 2.7 us)
Async XLA Ops:
  4.5 1.6 %copy-start = (bf16[4,64,4096]{2,1,0:T(8,128)(2,1)S(1)}, bf16[4,64,4096]{2,1,0:T(8,128)(2,1)}, u32[]{:S(2)}) copy-start(bf16[4,64,4096]{2,1,0:T(8,128)(2,1)} %reshape.63.x_ref) | copy-start | bytes 6291460
  11.2 12.4 %copy-start.4 = (s32[4096,1]{0,1:T(1,128)S(1)}, s32[4096,1]{0,1:T(1,128)}, u32[]{:S(2)}) copy-start(s32[4096,1]{0,1:T(1,128)} %param.6) | copy-start | bytes 49156
  12.5 23.3 %collective-permute-start = (bf16[16,16384]{1,0:T(8,128)(2,1)}, bf16[16,16384]{1,0:T(8,128)(2,1)}, u32[]{:S(2)}, u32[]{:S(2)}) collective-permute-start(bf16[16,16384]{1,0:T(8,128)(2,1)} %get-tuple-element.24), channel_id=1, source_target_pairs={{0,2},{2,4},{4,6},{6,8},{8,10},{10,12},{12,14},{14,16},{16,18},{18... | collective-permute-start | bytes 1572872 | tf_op jit(solution)/shard_map/ppermute | solution.py:395
  15.1 29.1 %collective-permute-start.1 = (bf16[16,16384]{1,0:T(8,128)(2,1)}, bf16[16,16384]{1,0:T(8,128)(2,1)}, u32[]{:S(2)}, u32[]{:S(2)}) collective-permute-start(bf16[16,16384]{1,0:T(8,128)(2,1)} %get-tuple-element.23), channel_id=1, source_target_pairs={{0,2},{2,4},{4,6},{6,8},{8,10},{10,12},{12,14},{14,16},{16,18},{18... | collective-permute-start | bytes 1572872 | tf_op jit(solution)/shard_map/ppermute | solution.py:395
  18.9 36.0 %collective-permute-start.2 = (bf16[16,16384]{1,0:T(8,128)(2,1)}, bf16[16,16384]{1,0:T(8,128)(2,1)S(1)}, u32[]{:S(2)}, u32[]{:S(2)}) collective-permute-start(bf16[16,16384]{1,0:T(8,128)(2,1)} %get-tuple-element.22), channel_id=1, source_target_pairs={{0,2},{2,4},{4,6},{6,8},{8,10},{10,12},{12,14},{14,16},{16,18},{18... | collective-permute-start | bytes 1572872 | tf_op jit(solution)/shard_map/ppermute | solution.py:395
  20.2 41.8 %collective-permute-start.3 = (bf16[16,16384]{1,0:T(8,128)(2,1)}, bf16[16,16384]{1,0:T(8,128)(2,1)S(1)}, u32[]{:S(2)}, u32[]{:S(2)}) collective-permute-start(bf16[16,16384]{1,0:T(8,128)(2,1)} %get-tuple-element.21), channel_id=1, source_target_pairs={{0,2},{2,4},{4,6},{6,8},{8,10},{10,12},{12,14},{14,16},{16,18},{18... | collective-permute-start | bytes 1572872 | tf_op jit(solution)/shard_map/ppermute | solution.py:395
  24.5 1.3 copy-start.3
  29.0 4.1 %copy-start.5 = (s32[4096]{0:T(1024)S(1)}, s32[4096]{0:T(1024)}, u32[]{:S(2)}) copy-start(s32[4096]{0:T(1024)} %param.7) | copy-start | bytes 49156
  33.1 2.7 %copy-start.1 = (bf16[272,2048]{1,0:T(8,128)(2,1)S(1)}, bf16[272,2048]{1,0:T(8,128)(2,1)}, u32[]{:S(2)}) copy-start(bf16[272,2048]{1,0:T(8,128)(2,1)} %constant.59.clone.cos_ref) | copy-start | bytes 3342340
  33.2 2.7 %copy-start.2 = (bf16[256,2048]{1,0:T(8,128)(2,1)S(1)}, bf16[256,2048]{1,0:T(8,128)(2,1)}, u32[]{:S(2)}) copy-start(bf16[256,2048]{1,0:T(8,128)(2,1)} %constant.60.clone.sin_ref) | copy-start | bytes 3145732
  43.4 30.9 %collective-permute-start.4 = (bf16[256,1024]{1,0:T(8,128)(2,1)S(1)}, bf16[256,1024]{1,0:T(8,128)(2,1)S(1)}, u32[]{:S(2)}, u32[]{:S(2)}) collective-permute-start(bf16[256,1024]{1,0:T(8,128)(2,1)S(1)} %get-tuple-element.17), channel_id=1, source_target_pairs={{0,1},{1,0},{2,3},{3,2},{4,5},{5,4},{6,7},{7,6},{8,9},{9,8},{10,11... | collective-permute-start | bytes 1572872 | tf_op jit(solution)/shard_map/ppermute | solution.py:402
  51.8 22.6 %collective-permute-start.5 = (bf16[256,1024]{1,0:T(8,128)(2,1)S(1)}, bf16[256,1024]{1,0:T(8,128)(2,1)S(1)}, u32[]{:S(2)}, u32[]{:S(2)}) collective-permute-start(bf16[256,1024]{1,0:T(8,128)(2,1)S(1)} %get-tuple-element.18), channel_id=1, source_target_pairs={{0,1},{1,0},{2,3},{3,2},{4,5},{5,4},{6,7},{7,6},{8,9},{9,8},{10,11... | collective-permute-start | bytes 1572872 | tf_op jit(solution)/shard_map/ppermute | solution.py:402
  61.4 21.0 %collective-permute-start.6 = (bf16[256,1024]{1,0:T(8,128)(2,1)S(1)}, bf16[256,1024]{1,0:T(8,128)(2,1)S(1)}, u32[]{:S(2)}, u32[]{:S(2)}) collective-permute-start(bf16[256,1024]{1,0:T(8,128)(2,1)S(1)} %get-tuple-element.19), channel_id=1, source_target_pairs={{0,1},{1,0},{2,3},{3,2},{4,5},{5,4},{6,7},{7,6},{8,9},{9,8},{10,11... | collective-permute-start | bytes 1572872 | tf_op jit(solution)/shard_map/ppermute | solution.py:402
  68.5 24.2 %collective-permute-start.7 = (bf16[256,1024]{1,0:T(8,128)(2,1)S(1)}, bf16[256,1024]{1,0:T(8,128)(2,1)S(1)}, u32[]{:S(2)}, u32[]{:S(2)}) collective-permute-start(bf16[256,1024]{1,0:T(8,128)(2,1)S(1)} %get-tuple-element.20), channel_id=1, source_target_pairs={{0,1},{1,0},{2,3},{3,2},{4,5},{5,4},{6,7},{7,6},{8,9},{9,8},{10,11... | collective-permute-start | bytes 1572872 | tf_op jit(solution)/shard_map/ppermute | solution.py:402

commit v4 on v3

v4 whole, which is shorter than its diff:
```python
import functools
import math

import jax
import jax.numpy as jnp
import numpy as np
from jax import lax
from jax.experimental import pallas as pl
from jax.experimental.pallas import tpu as pltpu
from jax.sharding import PartitionSpec as P

F = 2048
NFFT = 16384
LAGS = 512
HALF = LAGS // 2
WBAND = 128
STACKS_DEV = 128
CB = 64
SEGS = 8
PAIRS = CB * CB
CAP = 64
GROUP = 16
GROUPS = F // GROUP
WIDE = 128
VMEM = pl.BlockSpec(memory_space=pltpu.VMEM)
SMEM = pl.BlockSpec(memory_space=pltpu.SMEM)


def lag_rows(factor):
    bins = np.arange(1, F + 1)

    def phases(lags):
        wrapped = (np.asarray(lags)[:, None] * bins[None, :]) % NFFT
        return wrapped.astype(np.float32) * np.float32(2.0 * math.pi / NFFT)

    scale = np.float32(factor)
    last = np.zeros((16, F), np.float32)
    last[0] = np.cos(phases([HALF]))[0] * scale
    cos_rows = np.concatenate([np.cos(phases(np.arange(HALF))) * scale, last])
    sin_rows = np.sin(phases(np.concatenate([[HALF], np.arange(1, HALF)]))) * scale
    return cos_rows.astype(jnp.bfloat16), sin_rows.astype(jnp.bfloat16)


def whiten_kernel(x_ref, o_ref):
    lane = lax.broadcasted_iota(jnp.int32, (CB, WIDE), 1) // GROUP
    for band in range(F // WBAND):
        parts = []
        for part in range(2):
            first = part * F + band * WBAND
            parts.append([x_ref[s, :, first : first + WBAND].astype(jnp.float32) for s in range(4)])
        values = []
        scales = []
        for s in range(4):
            power = jnp.sum(parts[0][s] * parts[0][s] + parts[1][s] * parts[1][s], axis=1, keepdims=True)
            scales.append(lax.rsqrt(power * (1.0 / (2 * WBAND)) + 1e-06))
        for part in range(2):
            for s in range(4):
                values.append(parts[part][s] * scales[s])
        for step in (1, 2, 4):
            low = (lane // step) % 2 == 0
            swapped = list(values)
            for q in range(8):
                if q & step:
                    continue
                a, b = values[q], values[q + step]
                swapped[q] = jnp.where(low, a, pltpu.roll(b, GROUP * step, 1))
                swapped[q + step] = jnp.where(low, pltpu.roll(a, WIDE - GROUP * step, 1), b)
            values = swapped
        for g in range(8):
            first = (band * 8 + g) * WIDE
            o_ref[:, first : first + WIDE] = values[g].astype(jnp.bfloat16)


def whiten(spectra):
    return pl.pallas_call(
        whiten_kernel,
        out_shape=jax.ShapeDtypeStruct((CB, GROUPS * WIDE), jnp.bfloat16),
        in_specs=[VMEM],
        out_specs=VMEM,
        compiler_params=pltpu.CompilerParams(vmem_limit_bytes=12 * 2**20),
        cost_estimate=pl.CostEstimate(flops=20_000_000, bytes_accessed=2**22, transcendentals=4096),
        name="whiten",
    )(spectra.reshape(4, CB, 2 * F))


CHANS = 16
CHUNKS = CB // CHANS
CHUNK = CHANS * CB


def place_of(z, x, y, core):
    return ((z * 2 + x) * 4 + y) * 2 + core


def tile_kernel(
    own_ref, cos_ref, sin_ref, rows_ref,
    partner, g_re, g_im, keep, send, got, shift_send, shift_recv, swap_send, swap_recv,
):
    unroll = 32
    blk = lax.axis_index("blk")
    seg = lax.axis_index("seg")
    count = lax.axis_size("blk")
    ahead = ((blk + 1) % count, seg)
    behind = ((blk + count - 1) % count, seg)
    opposite = (blk, 1 - seg)
    barrier = pltpu.get_barrier_semaphore()
    for device in (ahead, behind, opposite):
        pl.semaphore_signal(barrier, inc=1, device_id=device, device_id_type=pl.DeviceIdType.MESH)
    pl.semaphore_wait(barrier, 3)

    def shift(j):
        at = pl.ds(pl.multiple_of(j * CHANS, CHANS), CHANS)
        return pltpu.make_async_remote_copy(
            src_ref=own_ref.at[at], dst_ref=partner.at[at],
            send_sem=shift_send.at[j], recv_sem=shift_recv.at[j],
            device_id=ahead, device_id_type=pl.DeviceIdType.MESH,
        )

    def swap(j):
        return pltpu.make_async_remote_copy(
            src_ref=send.at[j], dst_ref=got.at[j],
            send_sem=swap_send.at[j], recv_sem=swap_recv.at[j],
            device_id=opposite, device_id_type=pl.DeviceIdType.MESH,
        )

    for j in range(CHUNKS):
        shift(j).start()
    row = lax.broadcasted_iota(jnp.int32, (GROUP, WIDE), 0)
    lane = lax.broadcasted_iota(jnp.int32, (GROUP, WIDE), 1)
    kept = jnp.where(blk > 0, 1.0, 0.0)
    mask = jnp.where(row == lane % GROUP, kept, 0.0).astype(jnp.bfloat16)
    wide_lane = lax.broadcasted_iota(jnp.int32, (CB, WIDE), 1)
    turn = jnp.where(wide_lane < WIDE // 2, -1.0, 1.0).astype(jnp.bfloat16)
    top = lax.broadcasted_iota(jnp.int32, (HALF, 256), 0) == 0

    def chunk_step(j, carry):
        shift(j).wait()
        chan = pl.ds(pl.multiple_of(j * CHANS, CHANS), CHANS)

        def one(group):
            cols = pl.ds(pl.multiple_of(group * WIDE, WIDE), WIDE)
            own = own_ref[:, cols]
            turned = jnp.concatenate([own[:, CB:], own[:, :CB]], axis=1) * turn
            spread = jnp.broadcast_to(partner[chan, cols][:, None, :], (CHANS, GROUP, WIDE))
            out = lax.dot_general(
                (spread * mask[None]).reshape(CHANS * GROUP, WIDE),
                jnp.concatenate([own, turned], 0),
                (((1,), (1,)), ((), ())),
                preferred_element_type=jnp.float32,
            ).astype(jnp.bfloat16)
            rows = pl.ds(pl.multiple_of(group * GROUP, GROUP), GROUP)
            for i in range(CHANS // 2):
                first = out[2 * i * GROUP : (2 * i + 1) * GROUP]
                second = out[(2 * i + 1) * GROUP : (2 * i + 2) * GROUP]
                pair = slice(i * WIDE, (i + 1) * WIDE)
                g_re[rows, pair] = jnp.concatenate([first[:, :CB], second[:, :CB]], 1)
                g_im[rows, pair] = jnp.concatenate([first[:, CB:], second[:, CB:]], 1)

        def body(i, carry):
            for u in range(unroll):
                one(i * unroll + u)
            return carry

        lax.fori_loop(0, GROUPS // unroll, body, 0)
        for i in range(CHUNK // 256):
            cols = slice(i * 256, (i + 1) * 256)
            even = jnp.dot(cos_ref[...], g_re[:, cols], preferred_element_type=jnp.float32)
            odd = jnp.dot(sin_ref[...], g_im[:, cols], preferred_element_type=jnp.float32)
            low, last = even[:HALF], even[HALF : HALF + 1]
            before = jnp.where(top, last, low) + odd
            after = jnp.where(top, low, low - odd)
            keep[j, :, cols] = jnp.where(seg == 0, before, after)
            send[j, :, cols] = jnp.where(seg == 0, after, before).astype(jnp.bfloat16)
        swap(j).start()
        return carry

    lax.fori_loop(0, CHUNKS, chunk_step, 0)

    def finish_step(j, carry):
        swap(j).wait()
        for i in range(CHUNK // 256):
            cols = slice(i * 256, (i + 1) * 256)
            turned = (keep[j, :, cols] + got[j, :, cols].astype(jnp.float32)).T
            for side in range(2):
                at = pl.ds((j * CHUNK + i * 256) * 2 + side, 256, stride=2)
                rows_ref[at, :] = turned[:, side * WIDE : (side + 1) * WIDE]
        return carry

    lax.fori_loop(0, CHUNKS, finish_step, 0)


def tile_rows(own, cos_rows, sin_rows):
    return pl.pallas_call(
        tile_kernel,
        out_shape=jax.ShapeDtypeStruct((2 * PAIRS, WIDE), jnp.float32),
        in_specs=[VMEM, VMEM, VMEM],
        out_specs=VMEM,
        scratch_shapes=[
            pltpu.VMEM((CB, GROUPS * WIDE), jnp.bfloat16),
            pltpu.VMEM((F, CHUNK), jnp.bfloat16),
            pltpu.VMEM((F, CHUNK), jnp.bfloat16),
            pltpu.VMEM((CHUNKS, HALF, CHUNK), jnp.float32),
            pltpu.VMEM((CHUNKS, HALF, CHUNK), jnp.bfloat16),
            pltpu.VMEM((CHUNKS, HALF, CHUNK), jnp.bfloat16),
            pltpu.SemaphoreType.DMA((CHUNKS,)),
            pltpu.SemaphoreType.DMA((CHUNKS,)),
            pltpu.SemaphoreType.DMA((CHUNKS,)),
            pltpu.SemaphoreType.DMA((CHUNKS,)),
        ],
        compiler_params=pltpu.CompilerParams(
            collective_id=2, has_side_effects=True, vmem_limit_bytes=40 * 2**20
        ),
        cost_estimate=pl.CostEstimate(
            flops=25_000_000_000, bytes_accessed=2**24, transcendentals=0
        ),
        name="tiles",
    )(own, cos_rows, sin_rows)


def place_kernel(dest_ref, rows, out_ref, spread):
    def clear(i, carry):
        spread[pl.ds(pl.multiple_of(i * 512, 512), 512), :] = jnp.zeros((512, WIDE), jnp.float32)
        return carry

    lax.fori_loop(0, spread.shape[0] // 512, clear, 0)

    def move(i, carry):
        for u in range(64):
            p = i * 64 + u
            to = pl.multiple_of(dest_ref[p] * 2, 2)
            spread[pl.ds(to, 2), :] = rows[pl.ds(pl.multiple_of(p * 2, 2), 2), :]
        return carry

    lax.fori_loop(0, PAIRS // 64, move, 0)

    def finish(i, carry):
        at = pl.ds(pl.multiple_of(i * 512, 512), 512)
        out_ref[at, :] = spread[at, :].astype(jnp.bfloat16)
        return carry

    lax.fori_loop(0, spread.shape[0] // 512, finish, 0)


def place_rows(dest, rows, rows_out):
    return pl.pallas_call(
        place_kernel,
        out_shape=jax.ShapeDtypeStruct((2 * rows_out, WIDE), jnp.bfloat16),
        in_specs=[SMEM, VMEM],
        out_specs=VMEM,
        scratch_shapes=[pltpu.VMEM((2 * rows_out, WIDE), jnp.float32)],
        compiler_params=pltpu.CompilerParams(vmem_limit_bytes=24 * 2**20),
        name="place",
    )(dest, rows)


SLOTS_A, SLOTS_C, SLOTS_B = 48, 48, 32
AC = SLOTS_A + SLOTS_C


def reduce_kernel(
    rows_ref, slots_ref, out_ref,
    sib_rows, sib_slots, da, db, dc, ra, rb, rc, sa, sb, sc, ra2, rb2, rc2, t, tb, rt, rtb,
    send_sem, recv_sem,
):
    blk = lax.axis_index("blk")
    seg = lax.axis_index("seg")
    core = blk % 2
    y = (blk // 2) % 4
    x = (blk // 8) % 2
    z = blk // 16
    other = (place_of(z, x, y, 1 - core), seg)
    across = (place_of(z, 1 - x, y, core), seg)

    def along_y(k):
        return (place_of(z, x, (y + k) % 4, core), seg)

    def along_z(k):
        return (place_of((z + k) % 8, x, y, core), seg)

    partners = [other, across] + [along_y(k) for k in (1, 2, 3)] + [along_z(k) for k in range(1, 8)]
    barrier = pltpu.get_barrier_semaphore()
    for partner in partners:
        pl.semaphore_signal(barrier, inc=1, device_id=partner, device_id_type=pl.DeviceIdType.MESH)
    pl.semaphore_wait(barrier, len(partners))
    used = [0]

    def copy(src, dst, device):
        i = used[0]
        used[0] += 1
        made = pltpu.make_async_remote_copy(
            src_ref=src, dst_ref=dst, send_sem=send_sem.at[i], recv_sem=recv_sem.at[i],
            device_id=device, device_id_type=pl.DeviceIdType.MESH,
        )
        made.start()
        return made

    half = 2 * CB * CAP
    span = 2 * CAP
    order = [4, 3, 5, 2, 6, 1, 7, 0]
    named = copy(slots_ref.at[pl.ds((1 - core) * CB, CB)], sib_slots, other)
    swaps = {}
    for k in order:
        first = (z + k) % 8 * (8 * span)
        swaps[k] = copy(
            rows_ref.at[pl.ds((1 - core) * half + first, 8 * span)],
            sib_rows.at[pl.ds(first, 8 * span)],
            other,
        )
    named.wait()
    lane = lax.broadcasted_iota(jnp.int32, (1, 4 * CAP), 1)
    slot = lax.broadcasted_iota(jnp.int32, (STACKS_DEV, 4 * CAP), 0)

    def dense_one(i):
        zz, xx, yy = i // 8, (i // 4) % 2, i % 4
        names = jnp.concatenate([slots_ref[pl.ds(core * CB + i, 1), :], sib_slots[pl.ds(i, 1), :]], 1)
        left = jnp.where(lane % 2 == 0, names, -1)
        right = jnp.where(lane % 2 == 1, names, -1)
        hot = jnp.concatenate([slot == left, slot == right], 0)
        mine = rows_ref[pl.ds(pl.multiple_of(core * half + i * span, span), span), :]
        theirs = sib_rows[pl.ds(pl.multiple_of(i * span, span), span), :]
        total = jnp.dot(
            jnp.where(hot, 1.0, 0.0).astype(jnp.bfloat16),
            jnp.concatenate([mine, theirs], 0),
            preferred_element_type=jnp.float32,
        ).astype(jnp.bfloat16)
        total = jnp.concatenate([total[:STACKS_DEV], total[STACKS_DEV:]], 1)
        da[yy, zz, xx] = total[:SLOTS_A]
        dc[xx, zz, yy] = total[SLOTS_A:AC]
        db[zz, xx * 4 + yy] = total[AC:]

    def wide(value):
        return value.astype(jnp.float32)

    first_a, first_b, first_c, second_a, second_c, third = {}, {}, {}, {}, {}, {}
    for k in order:
        swaps[k].wait()
        there = (z + k) % 8

        def dense(i, carry, there=there):
            for u in range(4):
                dense_one(there * 8 + i * 4 + u)
            return carry

        lax.fori_loop(0, 2, dense, 0)
        first_c[k] = copy(dc.at[1 - x, there], rc.at[there], across)
        first_a[k] = [
            copy(da.at[(y + j) % 4, there], ra.at[j - 1, there], along_y(j)) for j in (2, 1, 3)
        ]
        if k:
            first_b[k] = copy(db.at[there], rb.at[k - 1], along_z(k))

    def second(k):
        there = (z + k) % 8
        first_c[k].wait()

        def sum_c(i, carry):
            sc[i, there] = (wide(dc[x, there, i]) + wide(rc[there, i])).astype(jnp.bfloat16)
            return carry

        lax.fori_loop(0, 4, sum_c, 0)
        second_c[k] = [
            copy(sc.at[(y + j) % 4, there], rc2.at[j - 1, there], along_y(j)) for j in (2, 1, 3)
        ]
        for made in first_a[k]:
            made.wait()

        def sum_a(i, carry):
            total = wide(da[y, there, i])
            for j in range(3):
                total += wide(ra[j, there, i])
            sa[i, there] = total.astype(jnp.bfloat16)
            return carry

        lax.fori_loop(0, 2, sum_a, 0)
        second_a[k] = copy(sa.at[1 - x, there], ra2.at[there], across)

    def finish(k):
        there = (z + k) % 8
        second_a[k].wait()
        t[there, :SLOTS_A] = (wide(sa[x, there]) + wide(ra2[there])).astype(jnp.bfloat16)
        for made in second_c[k]:
            made.wait()
        total = wide(sc[y, there])
        for j in range(3):
            total += wide(rc2[j, there])
        t[there, SLOTS_A:] = total.astype(jnp.bfloat16)
        if k:
            third[k] = copy(t.at[there], rt.at[k - 1], along_z(k))

    late = 2
    for n, k in enumerate(order):
        second(k)
        if n >= late:
            finish(order[n - late])
    for made in first_b.values():
        made.wait()

    def sum_b(i, carry):
        total = wide(db[z, i])
        for k in range(7):
            total += wide(rb[k, i])
        sb[i % 4, i // 4] = total.astype(jnp.bfloat16)
        return carry

    lax.fori_loop(0, 8, sum_b, 0)
    second_b = [copy(sb.at[(y + k) % 4], rb2.at[k - 1], along_y(k)) for k in (1, 2, 3)]
    for k in order[-late:]:
        finish(k)
    for made in second_b:
        made.wait()

    def sum_b2(i, carry):
        total = wide(sb[y, i])
        for k in range(3):
            total += wide(rb2[k, i])
        tb[i] = total.astype(jnp.bfloat16)
        return carry

    lax.fori_loop(0, 2, sum_b2, 0)
    third_b = copy(tb.at[1 - x], rtb, across)
    total = wide(t[z])
    for k in order[:-1]:
        third[k].wait()
        total += wide(rt[k - 1])
    out_ref[:AC, :] = total
    third_b.wait()
    out_ref[AC:, :] = wide(tb[x]) + wide(rtb[...])


def reduce_rows(rows, slots):
    def buf(*shape):
        return pltpu.VMEM((*shape, HALF), jnp.bfloat16)

    a, b, c = SLOTS_A, SLOTS_B, SLOTS_C
    count = 9 + 8 + 24 + 7 + 24 + 8 + 7 + 3 + 1
    return pl.pallas_call(
        reduce_kernel,
        out_shape=jax.ShapeDtypeStruct((STACKS_DEV, HALF), jnp.float32),
        in_specs=[VMEM, VMEM],
        out_specs=VMEM,
        scratch_shapes=[
            pltpu.VMEM((2 * CB * CAP, WIDE), jnp.bfloat16), pltpu.VMEM((CB, STACKS_DEV), jnp.int32),
            buf(4, 8, 2, a), buf(8, 8, b), buf(2, 8, 4, c), buf(3, 8, 2, a), buf(7, 8, b), buf(8, 4, c),
            buf(2, 8, a), buf(4, 2, b), buf(4, 8, c), buf(8, a), buf(3, 2, b), buf(3, 8, c),
            buf(8, AC), buf(2, b), buf(7, AC), buf(b),
            pltpu.SemaphoreType.DMA((count,)), pltpu.SemaphoreType.DMA((count,)),
        ],
        compiler_params=pltpu.CompilerParams(
            collective_id=1, has_side_effects=True, vmem_limit_bytes=40 * 2**20
        ),
        cost_estimate=pl.CostEstimate(flops=2_000_000_000, bytes_accessed=2**23, transcendentals=0),
        name="reduce_rows",
    )(rows, slots)


def local(spectra, owner_device, stack_slot):
    blk_devices = lax.axis_size("blk")
    seg = lax.axis_index("seg")
    factor = (2.0 * F * SEGS) ** (-0.5)
    cos_rows, sin_rows = lag_rows(factor)
    rows = tile_rows(whiten(spectra), cos_rows, sin_rows)
    owner_rows = owner_device[:, 0]
    ordered = (owner_rows % 2) * CB + owner_rows // 2
    hot = ordered[:, None] == lax.iota(jnp.int32, blk_devices)[None, :]
    count = hot.astype(jnp.int32)
    position = jnp.sum((jnp.cumsum(count, axis=0) - count) * count, axis=1)
    place_hot = position[:, None] == lax.iota(jnp.int32, STACKS_DEV)[None, :] // 2
    named = jnp.where(place_hot, (stack_slot + 1)[:, None], 0).astype(jnp.bfloat16)
    slots = lax.dot_general(
        hot.astype(jnp.bfloat16), named, (((0,), (0,)), ((), ())), preferred_element_type=jnp.float32
    )
    slots = slots.astype(jnp.int32) - 1
    outgoing = place_rows(ordered * CAP + position, rows, blk_devices * CAP)
    stacks = reduce_rows(outgoing, slots)
    lags = lax.iota(jnp.int32, HALF)
    turned = jnp.roll(stacks[:, ::-1], 1, axis=1)
    stacks = jnp.where(seg == 0, turned, stacks)
    return stacks.astype(jnp.bfloat16)


def solution(mesh):
    placed = (P("seg", "blk", None, None), P("blk", None), P("blk"))
    return jax.shard_map(
        local, mesh=mesh, in_specs=placed, out_specs=P("blk", "seg"), check_vma=False
    )
```

time: 159 us -> 143 us (0.90)
  Pallas kernels: 97.8 us -> 131 us
  starting transfers between devices: 18.9 us -> 0 us
  waiting for transfers between devices: 18.4 us -> 0 us
  local copies, waits for them, and re-layouts: 13.4 us -> 5.05 us
  other arithmetic: 7.34 us -> 4.1 us
    pallas_call x5 -> x2, Pallas kernels: 35.9 us -> 71.5 us  [the longest x1 64.9 us: tile_rows(): pl.pallas_call(tile_kernel, out_shape=jax.ShapeDtypeStruct((2 * PAIRS, WI...]
    ppermute x8 -> x0, starting transfers between devices: 18.9 us -> none  [the longest x4 11 us: local(): lax.ppermute(whitened[i * chans:(i + 1) * chans], 'blk', ahead)]
    ppermute x8 -> x0, waiting for transfers between devices: 18.4 us -> none  [the longest x4 18.4 us: local(): gots.append(lax.ppermute(send, 'seg', [(0, 1), (1, 0)]))]
    another operation x3, local copies, waits for them, and re-layouts: 4.15 us -> 1.23 us
    another operation x3, other arithmetic: 3.82 us -> 0.89 us
    unnamed x14 -> x10, local copies, waits for them, and re-layouts: 3.24 us -> 0.35 us
    pallas_call x1, Pallas kernels: 56.7 us -> 53.9 us  [reduce_rows(): pl.pallas_call(reduce_kernel, out_shape=jax.ShapeDtypeStruct((STACKS_DEV,...]
  transfers between devices with their start and end apart: 8 -> 0, of which waited for: 2 -> 0; matrix products, arithmetic and copies ran while one was open for 8% -> 0% of each run, Pallas kernels for 18% -> 0%
where the time goes in v4:
time: 143 us; the launch traced here: 142 us
  Pallas kernels  131 us (92%)
  local copies, waits for them, and re-layouts  5.05 us (4%)
  other arithmetic  4.1 us (3%)
  matrix products  2.44 us (2%)
    pallas_call x1, Pallas kernels, tile_rows(): pl.pallas_call(tile_kernel, out_shape=jax.ShapeDtypeStruct((2 * PAIRS, WI...  64.9 us
    pallas_call x1, Pallas kernels, reduce_rows(): pl.pallas_call(reduce_kernel, out_shape=jax.ShapeDtypeStruct((STACKS_DEV,...  53.9 us
    pallas_call x1, Pallas kernels, place_rows(): pl.pallas_call(place_kernel, out_shape=jax.ShapeDtypeStruct((2 * rows_out...  6.6 us
    pallas_call x1, Pallas kernels, whiten(): pl.pallas_call(whiten_kernel, out_shape=jax.ShapeDtypeStruct((CB, GROUPS...  5.1 us
    reshape x1, local copies, waits for them, and re-layouts, whiten(): spectra.reshape(4, CB, 2 * F)  3.29 us

profile of v4, /device:TPU:4, one launch (start us, length us, event | category | flops | bytes accessed | tf_op | source)
XLA Modules:
  0.0 142.3 jit_solution(4657379239402601620)
XLA Ops:
  0.0 0.8 fusion.19
  0.8 0.1 copy.7
  0.9 0.6 fusion.2
  1.6 0.1 reduce-window.9
  1.6 0.2 broadcast_add_fusion
  1.9 1.2 copy.8
  3.1 0.0 copy-start.2
  3.1 1.6 %fusion.1 = s32[4096]{0:T(1024)S(1)} fusion(s32[128,32,128]{0,2,1:T(8,128)S(1)} %copy.8, s32[4096]{0:T(1024)S(1)} %bitcast.16), kind=kLoop, calls=%fused_computation.2 | loop fusion | flops 2617344 | bytes 2129920 | tf_op jit(solution)/shard_map/reduce_sum | solution.py:466
  4.7 0.0 copy-done.2
  4.8 3.3 %reshape.59.x_ref = bf16[4,64,4096]{2,1,0:T(8,128)(2,1)S(1)} reshape(bf16[4,64,2,2048]{3,2,1,0:T(2,128)(2,1)} %param.5) | data formatting | bytes 4194304 | tf_op jit(solution)/shard_map/reshape | solution.py:83
  8.1 0.0 copy-start
  8.1 0.0 copy-start.1
  8.1 5.1 %whiten.1.own_ref = bf16[64,16384]{1,0:T(8,128)(2,1)S(1)} custom-call(bf16[4,64,4096]{2,1,0:T(8,128)(2,1)S(1)} %reshape.59.x_ref), custom_call_target="tpu_custom_call" | custom-call | flops 20000000 | bytes 4194304 | tf_op jit(solution)/shard_map/whiten/pallas_call | solution.py:75
  13.2 0.0 copy-done
  13.2 0.0 copy-done.1
  13.2 64.9 %tiles.1.rows = f32[8192,128]{1,0:T(8,128)S(1)} custom-call(bf16[64,16384]{1,0:T(8,128)(2,1)S(1)} %whiten.1.own_ref, bf16[272,2048]{1,0:T(8,128)(2,1)S(1)} %copy-done, bf16[256,2048]{1,0:T(8,128)(2,1)S(1)} %copy-done.1), custom_call_target="tpu_custom_call" | custom-call | flops 24999999488 | bytes 16777216 | tf_op jit(solution)/shard_map/tiles/pallas_call | solution.py:193
  78.1 0.0 copy-start.3
  78.1 6.6 %place.1.rows_ref = bf16[16384,128]{1,0:T(8,128)(2,1)S(1)} custom-call(s32[4096]{0:T(1024)S(1)} %fusion.17.dest_ref, f32[8192,128]{1,0:T(8,128)S(1)} %tiles.1.rows), custom_call_target="tpu_custom_call" | custom-call | tf_op jit(solution)/shard_map/place/pallas_call | solution.py:245
  84.8 2.4 %fusion.6.slots_ref = s32[128,128]{1,0:T(8,128)S(1)} fusion(s32[4096]{0:T(1024)S(1)} %broadcast_add_fusion.1, s32[128]{0:T(128)S(1)} %and_select_fusion.2, s32[4096]{0:T(1024)S(1)} %bitcast.17, s32[4096]{0:T(1024)S(1)} %fusion.1), kind=kOutput, calls=%fused_computation.10 | convolution fusion | flops 136347648 | bytes 115200 | tf_op jit(solution)/shard_map/dot_general | solution.py:469
  87.2 53.9 %reduce_rows.1 = f32[128,256]{1,0:T(8,128)S(1)} custom-call(bf16[16384,128]{1,0:T(8,128)(2,1)S(1)} %place.1.rows_ref, s32[128,128]{1,0:T(8,128)S(1)} %fusion.6.slots_ref), custom_call_target="tpu_custom_call" | custom-call | flops 2000000000 | bytes 8388608 | tf_op jit(solution)/shard_map/reduce_rows/pallas_call | solution.py:436
  141.2 0.1 slice.21
  141.3 0.2 reverse.2
  141.5 0.1 slice.26
  141.6 0.7 fusion.13
  (7 shorter events, 0.0 us)
Async XLA Ops:
  3.1 1.6 %copy-start.2 = (s32[4096,1]{0,1:T(1,128)S(1)}, s32[4096,1]{0,1:T(1,128)}, u32[]{:S(2)}) copy-start(s32[4096,1]{0,1:T(1,128)} %param.6) | copy-start | bytes 49156
  8.1 5.1 %copy-start = (bf16[272,2048]{1,0:T(8,128)(2,1)S(1)}, bf16[272,2048]{1,0:T(8,128)(2,1)}, u32[]{:S(2)}) copy-start(bf16[272,2048]{1,0:T(8,128)(2,1)} %constant.57.clone.cos_ref) | copy-start | bytes 3342340
  8.1 5.1 %copy-start.1 = (bf16[256,2048]{1,0:T(8,128)(2,1)S(1)}, bf16[256,2048]{1,0:T(8,128)(2,1)}, u32[]{:S(2)}) copy-start(bf16[256,2048]{1,0:T(8,128)(2,1)} %constant.58.clone.sin_ref) | copy-start | bytes 3145732
  78.1 6.6 %copy-start.3 = (s32[4096]{0:T(1024)S(1)}, s32[4096]{0:T(1024)}, u32[]{:S(2)}) copy-start(s32[4096]{0:T(1024)} %param.7) | copy-start | bytes 49156

commit v5 on v4

--- a/solution.py
+++ b/solution.py
@@ -93,8 +93,8 @@
 
 
 def tile_kernel(
-    own_ref, cos_ref, sin_ref, rows_ref,
-    partner, g_re, g_im, keep, send, got, shift_send, shift_recv, swap_send, swap_recv,
+    own_ref, cos_ref, sin_ref, owner_ref, slot_ref, rows_ref, dest_ref, slots_ref,
+    partner, g_re, g_im, keep, send, got, passing, shift_send, shift_recv, swap_send, swap_recv, pass_send, pass_recv,
 ):
     unroll = 32
     blk = lax.axis_index("blk")
@@ -103,10 +103,57 @@
     ahead = ((blk + 1) % count, seg)
     behind = ((blk + count - 1) % count, seg)
     opposite = (blk, 1 - seg)
+    core = blk % 2
+    y = (blk // 2) % 4
+    x = (blk // 8) % 2
+    z = blk // 16
+    turns = jnp.logical_and(y == 3, core == 1)
+    lands = jnp.logical_and(y == 0, core == 0)
+    relays = jnp.logical_and(jnp.logical_or(y == 1, y == 2), core == 1)
+    origin = place_of(z, x, 3, 1)
+    target = ((origin + 1) % count, seg)
+    back = (blk + count - 1) % count
     barrier = pltpu.get_barrier_semaphore()
+
+    def greet(device):
+        pl.semaphore_signal(barrier, inc=1, device_id=device, device_id_type=pl.DeviceIdType.MESH)
+
     for device in (ahead, behind, opposite):
-        pl.semaphore_signal(barrier, inc=1, device_id=device, device_id_type=pl.DeviceIdType.MESH)
-    pl.semaphore_wait(barrier, 3)
+        greet(device)
+
+    @pl.when(turns)
+    def _():
+        greet((place_of(z, x, 1, 1), seg))
+        greet((place_of(z, x, 2, 1), seg))
+
+    @pl.when(relays)
+    def _():
+        greet((origin, seg))
+        greet(target)
+
+    @pl.when(lands)
+    def _():
+        greet((place_of(back // 16, (back // 8) % 2, 1, 1), seg))
+        greet((place_of(back // 16, (back // 8) % 2, 2, 1), seg))
+
+    special = jnp.logical_or(jnp.logical_or(turns, lands), relays)
+    pl.semaphore_wait(barrier, jnp.where(special, 5, 3))
+
+    def detour(j):
+        at = pl.ds(pl.multiple_of(j * CHANS, CHANS), CHANS)
+        return pltpu.make_async_remote_copy(
+            src_ref=own_ref.at[at], dst_ref=passing,
+            send_sem=shift_send.at[j], recv_sem=pass_recv,
+            device_id=(place_of(z, x, j - 1, 1), seg), device_id_type=pl.DeviceIdType.MESH,
+        )
+
+    def forward(j):
+        at = pl.ds(pl.multiple_of(j * CHANS, CHANS), CHANS)
+        return pltpu.make_async_remote_copy(
+            src_ref=passing, dst_ref=partner.at[at],
+            send_sem=pass_send, recv_sem=shift_recv.at[j],
+            device_id=target, device_id_type=pl.DeviceIdType.MESH,
+        )
 
     def shift(j):
         at = pl.ds(pl.multiple_of(j * CHANS, CHANS), CHANS)
@@ -123,8 +170,26 @@
             device_id=opposite, device_id_type=pl.DeviceIdType.MESH,
         )
 
-    for j in range(CHUNKS):
+    @pl.when(turns)
+    def _():
+        for j in range(CHUNKS // 2, CHUNKS):
+            detour(j).start()
+
+    for j in range(CHUNKS // 2):
         shift(j).start()
+
+    @pl.when(jnp.logical_not(turns))
+    def _():
+        for j in range(CHUNKS // 2, CHUNKS):
+            shift(j).start()
+
+    for j in range(CHUNKS // 2, CHUNKS):
+
+        @pl.when(jnp.logical_and(relays, y == j - 1))
+        def _(j=j):
+            detour(j).wait_recv()
+            forward(j).start()
+
     row = lax.broadcasted_iota(jnp.int32, (GROUP, WIDE), 0)
     lane = lax.broadcasted_iota(jnp.int32, (GROUP, WIDE), 1)
     kept = jnp.where(blk > 0, 1.0, 0.0)
@@ -176,6 +241,37 @@
 
     lax.fori_loop(0, CHUNKS, chunk_step, 0)
 
+    row_of = lax.broadcasted_iota(jnp.int32, (256, 256), 0)
+    upper = jnp.where(row_of < lax.broadcasted_iota(jnp.int32, (256, 256), 1), 1.0, 0.0)
+    upper = upper.astype(jnp.bfloat16)
+    owner_row = lax.broadcasted_iota(jnp.int32, (STACKS_DEV, 256), 0)
+
+    def index_step(i, carry):
+        seen, named = carry
+        at = pl.ds(pl.multiple_of(i * 256, 256), 256)
+        owner = owner_ref[:, at]
+        ordered = owner % 2 * CB + owner // 2
+        hot = jnp.where(owner_row == ordered, 1.0, 0.0)
+        before = jnp.dot(hot.astype(jnp.bfloat16), upper, preferred_element_type=jnp.float32) + seen
+        position = jnp.sum(hot * before, axis=0, keepdims=True).astype(jnp.int32)
+        dest_ref[:, at] = ordered * CAP + position
+        names = jnp.where(owner_row // 2 == position, (slot_ref[:, at] + 1).astype(jnp.float32), 0.0)
+        named += lax.dot_general(
+            hot.astype(jnp.bfloat16),
+            names.astype(jnp.bfloat16),
+            (((1,), (1,)), ((), ())),
+            preferred_element_type=jnp.float32,
+        )
+        return seen + jnp.sum(hot, axis=1, keepdims=True), named
+
+    _, named = lax.fori_loop(
+        0,
+        PAIRS // 256,
+        index_step,
+        (jnp.zeros((STACKS_DEV, 1), jnp.float32), jnp.zeros((STACKS_DEV, STACKS_DEV), jnp.float32)),
+    )
+    slots_ref[...] = named.astype(jnp.int32) - 1
+
     def finish_step(j, carry):
         swap(j).wait()
         for i in range(CHUNK // 256):
@@ -187,14 +283,23 @@
         return carry
 
     lax.fori_loop(0, CHUNKS, finish_step, 0)
-
-
-def tile_rows(own, cos_rows, sin_rows):
+    for j in range(CHUNKS // 2, CHUNKS):
+
+        @pl.when(jnp.logical_and(relays, y == j - 1))
+        def _(j=j):
+            forward(j).wait_send()
+
+
+def tile_rows(own, cos_rows, sin_rows, owner, slot):
     return pl.pallas_call(
         tile_kernel,
-        out_shape=jax.ShapeDtypeStruct((2 * PAIRS, WIDE), jnp.float32),
-        in_specs=[VMEM, VMEM, VMEM],
-        out_specs=VMEM,
+        out_shape=(
+            jax.ShapeDtypeStruct((2 * PAIRS, WIDE), jnp.float32),
+            jax.ShapeDtypeStruct((1, PAIRS), jnp.int32),
+            jax.ShapeDtypeStruct((STACKS_DEV, STACKS_DEV), jnp.int32),
+        ),
+        in_specs=[VMEM] * 5,
+        out_specs=(VMEM, VMEM, VMEM),
         scratch_shapes=[
             pltpu.VMEM((CB, GROUPS * WIDE), jnp.bfloat16),
             pltpu.VMEM((F, CHUNK), jnp.bfloat16),
@@ -202,10 +307,13 @@
             pltpu.VMEM((CHUNKS, HALF, CHUNK), jnp.float32),
             pltpu.VMEM((CHUNKS, HALF, CHUNK), jnp.bfloat16),
             pltpu.VMEM((CHUNKS, HALF, CHUNK), jnp.bfloat16),
+            pltpu.VMEM((CHANS, GROUPS * WIDE), jnp.bfloat16),
             pltpu.SemaphoreType.DMA((CHUNKS,)),
             pltpu.SemaphoreType.DMA((CHUNKS,)),
             pltpu.SemaphoreType.DMA((CHUNKS,)),
             pltpu.SemaphoreType.DMA((CHUNKS,)),
+            pltpu.SemaphoreType.DMA,
+            pltpu.SemaphoreType.DMA,
         ],
         compiler_params=pltpu.CompilerParams(
             collective_id=2, has_side_effects=True, vmem_limit_bytes=40 * 2**20
@@ -214,7 +322,7 @@
             flops=25_000_000_000, bytes_accessed=2**24, transcendentals=0
         ),
         name="tiles",
-    )(own, cos_rows, sin_rows)
+    )(own, cos_rows, sin_rows, owner, slot)
 
 
 def place_kernel(dest_ref, rows, out_ref, spread):
@@ -458,19 +566,14 @@
     seg = lax.axis_index("seg")
     factor = (2.0 * F * SEGS) ** (-0.5)
     cos_rows, sin_rows = lag_rows(factor)
-    rows = tile_rows(whiten(spectra), cos_rows, sin_rows)
-    owner_rows = owner_device[:, 0]
-    ordered = (owner_rows % 2) * CB + owner_rows // 2
-    hot = ordered[:, None] == lax.iota(jnp.int32, blk_devices)[None, :]
-    count = hot.astype(jnp.int32)
-    position = jnp.sum((jnp.cumsum(count, axis=0) - count) * count, axis=1)
-    place_hot = position[:, None] == lax.iota(jnp.int32, STACKS_DEV)[None, :] // 2
-    named = jnp.where(place_hot, (stack_slot + 1)[:, None], 0).astype(jnp.bfloat16)
-    slots = lax.dot_general(
-        hot.astype(jnp.bfloat16), named, (((0,), (0,)), ((), ())), preferred_element_type=jnp.float32
+    rows, dest, slots = tile_rows(
+        whiten(spectra),
+        cos_rows,
+        sin_rows,
+        owner_device.reshape(1, PAIRS),
+        stack_slot.reshape(1, PAIRS),
     )
-    slots = slots.astype(jnp.int32) - 1
-    outgoing = place_rows(ordered * CAP + position, rows, blk_devices * CAP)
+    outgoing = place_rows(dest.reshape(PAIRS), rows, blk_devices * CAP)
     stacks = reduce_rows(outgoing, slots)
     lags = lax.iota(jnp.int32, HALF)
     turned = jnp.roll(stacks[:, ::-1], 1, axis=1)

time: 143 us -> 132 us (0.923)
  Pallas kernels: 131 us -> 127 us
  other arithmetic: 4.1 us -> 0.72 us
  matrix products: 2.44 us -> 0 us
    pallas_call x1, Pallas kernels: 53.9 us -> 50.3 us  [reduce_rows(): pl.pallas_call(reduce_kernel, out_shape=jax.ShapeDtypeStruct((STACKS_DEV,...]
    dot_general x1 -> x0, matrix products: 2.44 us -> none  [local(): lax.dot_general(hot.astype(jnp.bfloat16), named, (((0,), (0,)), ((), ()))...]
    reduce_sum x1 -> x0, other arithmetic: 1.61 us -> none  [local(): position = jnp.sum((jnp.cumsum(count, axis=0) - count) * count, axis=1)]
where the time goes in v5:
time: 132 us
  Pallas kernels  127 us (96%)
  local copies, waits for them, and re-layouts  3.72 us (3%)
    pallas_call x1, Pallas kernels, tile_rows(): pl.pallas_call(tile_kernel, out_shape=(jax.ShapeDtypeStruct((2 * PAIRS, W...  65.2 us
    pallas_call x1, Pallas kernels, reduce_rows(): pl.pallas_call(reduce_kernel, out_shape=jax.ShapeDtypeStruct((STACKS_DEV,...  50.3 us
    pallas_call x1, Pallas kernels, place_rows(): pl.pallas_call(place_kernel, out_shape=jax.ShapeDtypeStruct((2 * rows_out...  6.6 us
    pallas_call x1, Pallas kernels, whiten(): pl.pallas_call(whiten_kernel, out_shape=jax.ShapeDtypeStruct((CB, GROUPS...  5.1 us
    reshape x1, local copies, waits for them, and re-layouts, whiten(): spectra.reshape(4, CB, 2 * F)  3.28 us

profile of v5, /device:TPU:4, one launch (start us, length us, event | category | flops | bytes accessed | tf_op | source)
XLA Modules:
  0.0 131.7 jit_solution(15409077869514412705)
XLA Ops:
  0.0 3.3 %reshape.12.x_ref = bf16[4,64,4096]{2,1,0:T(8,128)(2,1)S(1)} reshape(bf16[4,64,2,2048]{3,2,1,0:T(2,128)(2,1)} %param.5) | data formatting | bytes 4194304 | tf_op jit(solution)/shard_map/reshape | solution.py:83
  3.3 0.0 copy-start
  3.3 0.0 copy-start.1
  3.3 0.0 copy-start.2
  3.3 0.0 copy-start.3
  3.3 5.1 %whiten.1.own_ref = bf16[64,16384]{1,0:T(8,128)(2,1)S(1)} custom-call(bf16[4,64,4096]{2,1,0:T(8,128)(2,1)S(1)} %reshape.12.x_ref), custom_call_target="tpu_custom_call" | custom-call | flops 20000000 | bytes 4194304 | tf_op jit(solution)/shard_map/whiten/pallas_call | solution.py:75
  8.4 0.0 copy-done
  8.5 0.0 copy-done.1
  8.5 0.0 copy-done.2
  8.5 0.0 copy-done.3
  8.5 65.2 %tiles.1 = (f32[8192,128]{1,0:T(8,128)S(1)}, s32[1,4096]{1,0:T(1,128)S(1)}, s32[128,128]{1,0:T(8,128)S(1)}) custom-call(bf16[64,16384]{1,0:T(8,128)(2,1)S(1)} %whiten.1.own_ref, bf16[272,2048]{1,0:T(8,128)(2,1)S(1)} %copy-done.2, bf16[256,2048]{1,0:T(8,128)(2,1)S(1)} %copy-done.3, s32[1,4096]{1,0:T(1,128)S(1)} %bitcast.5, s32[1,4096]{1,0:T(1,128)S(1)} %bitcast.6), custom_call_target="tpu_custom_call" | custom-call | flops 24999999488 | bytes 16777216 | tf_op jit(solution)/shard_map/tiles/pallas_call | solution.py:294
  73.7 6.6 %place.1.rows_ref = bf16[16384,128]{1,0:T(8,128)(2,1)S(1)} custom-call(s32[4096]{0:T(1024)S(1)} %bitcast.4, f32[8192,128]{1,0:T(8,128)S(1)} %get-tuple-element.9.rows), custom_call_target="tpu_custom_call" | custom-call | tf_op jit(solution)/shard_map/place/pallas_call | solution.py:353
  80.3 50.3 %reduce_rows.1 = f32[128,256]{1,0:T(8,128)S(1)} custom-call(bf16[16384,128]{1,0:T(8,128)(2,1)S(1)} %place.1.rows_ref, s32[128,128]{1,0:T(8,128)S(1)} %get-tuple-element.10.slots_ref), custom_call_target="tpu_custom_call" | custom-call | flops 2000000000 | bytes 8388608 | tf_op jit(solution)/shard_map/reduce_rows/pallas_call | solution.py:544
  130.6 0.1 slice.13
  130.7 0.2 reverse.2
  130.9 0.1 slice.15
  131.0 0.7 fusion
  (1 shorter events, 0.0 us)
Async XLA Ops:
  3.3 5.2 %copy-start = (s32[4096,1]{0,1:T(1,128)S(1)}, s32[4096,1]{0,1:T(1,128)}, u32[]{:S(2)}) copy-start(s32[4096,1]{0,1:T(1,128)} %param.6) | copy-start | bytes 49156
  3.3 5.2 %copy-start.1 = (s32[4096]{0:T(1024)S(1)}, s32[4096]{0:T(1024)}, u32[]{:S(2)}) copy-start(s32[4096]{0:T(1024)} %param.7) | copy-start | bytes 49156
  3.3 5.2 %copy-start.2 = (bf16[272,2048]{1,0:T(8,128)(2,1)S(1)}, bf16[272,2048]{1,0:T(8,128)(2,1)}, u32[]{:S(2)}) copy-start(bf16[272,2048]{1,0:T(8,128)(2,1)} %constant.10.clone.cos_ref) | copy-start | bytes 3342340
  3.3 5.2 %copy-start.3 = (bf16[256,2048]{1,0:T(8,128)(2,1)S(1)}, bf16[256,2048]{1,0:T(8,128)(2,1)}, u32[]{:S(2)}) copy-start(bf16[256,2048]{1,0:T(8,128)(2,1)} %constant.11.clone.sin_ref) | copy-start | bytes 3145732

commit v6 on v5

--- a/solution.py
+++ b/solution.py
@@ -144,7 +144,7 @@
         return pltpu.make_async_remote_copy(
             src_ref=own_ref.at[at], dst_ref=passing,
             send_sem=shift_send.at[j], recv_sem=pass_recv,
-            device_id=(place_of(z, x, j - 1, 1), seg), device_id_type=pl.DeviceIdType.MESH,
+            device_id=(place_of(z, x, 4 - j, 1), seg), device_id_type=pl.DeviceIdType.MESH,
         )
 
     def forward(j):
@@ -185,7 +185,7 @@
 
     for j in range(CHUNKS // 2, CHUNKS):
 
-        @pl.when(jnp.logical_and(relays, y == j - 1))
+        @pl.when(jnp.logical_and(relays, y == 4 - j))
         def _(j=j):
             detour(j).wait_recv()
             forward(j).start()
@@ -234,9 +234,11 @@
             low, last = even[:HALF], even[HALF : HALF + 1]
             before = jnp.where(top, last, low) + odd
             after = jnp.where(top, low, low - odd)
-            keep[j, :, cols] = jnp.where(seg == 0, before, after)
-            send[j, :, cols] = jnp.where(seg == 0, after, before).astype(jnp.bfloat16)
-        swap(j).start()
+            piece, part = j * 2 + i // 2, slice(i % 2 * 256, (i % 2 + 1) * 256)
+            keep[piece, :, part] = jnp.where(seg == 0, before, after)
+            send[piece, :, part] = jnp.where(seg == 0, after, before).astype(jnp.bfloat16)
+            if i % 2 == 1:
+                swap(piece).start()
         return carry
 
     lax.fori_loop(0, CHUNKS, chunk_step, 0)
@@ -274,18 +276,18 @@
 
     def finish_step(j, carry):
         swap(j).wait()
-        for i in range(CHUNK // 256):
+        for i in range(2):
             cols = slice(i * 256, (i + 1) * 256)
             turned = (keep[j, :, cols] + got[j, :, cols].astype(jnp.float32)).T
             for side in range(2):
-                at = pl.ds((j * CHUNK + i * 256) * 2 + side, 256, stride=2)
+                at = pl.ds((j * 2 + i) * 512 + side, 256, stride=2)
                 rows_ref[at, :] = turned[:, side * WIDE : (side + 1) * WIDE]
         return carry
 
-    lax.fori_loop(0, CHUNKS, finish_step, 0)
+    lax.fori_loop(0, 2 * CHUNKS, finish_step, 0)
     for j in range(CHUNKS // 2, CHUNKS):
 
-        @pl.when(jnp.logical_and(relays, y == j - 1))
+        @pl.when(jnp.logical_and(relays, y == 4 - j))
         def _(j=j):
             forward(j).wait_send()
 
@@ -304,14 +306,14 @@
             pltpu.VMEM((CB, GROUPS * WIDE), jnp.bfloat16),
             pltpu.VMEM((F, CHUNK), jnp.bfloat16),
             pltpu.VMEM((F, CHUNK), jnp.bfloat16),
-            pltpu.VMEM((CHUNKS, HALF, CHUNK), jnp.float32),
-            pltpu.VMEM((CHUNKS, HALF, CHUNK), jnp.bfloat16),
-            pltpu.VMEM((CHUNKS, HALF, CHUNK), jnp.bfloat16),
+            pltpu.VMEM((2 * CHUNKS, HALF, CHUNK // 2), jnp.float32),
+            pltpu.VMEM((2 * CHUNKS, HALF, CHUNK // 2), jnp.bfloat16),
+            pltpu.VMEM((2 * CHUNKS, HALF, CHUNK // 2), jnp.bfloat16),
             pltpu.VMEM((CHANS, GROUPS * WIDE), jnp.bfloat16),
             pltpu.SemaphoreType.DMA((CHUNKS,)),
             pltpu.SemaphoreType.DMA((CHUNKS,)),
-            pltpu.SemaphoreType.DMA((CHUNKS,)),
-            pltpu.SemaphoreType.DMA((CHUNKS,)),
+            pltpu.SemaphoreType.DMA((2 * CHUNKS,)),
+            pltpu.SemaphoreType.DMA((2 * CHUNKS,)),
             pltpu.SemaphoreType.DMA,
             pltpu.SemaphoreType.DMA,
         ],

time: 132 us -> 130 us (0.985)
  Pallas kernels: 127 us -> 125 us
    pallas_call x1, Pallas kernels: 50.3 us -> 48.7 us  [reduce_rows(): pl.pallas_call(reduce_kernel, out_shape=jax.ShapeDtypeStruct((STACKS_DEV,...]
where the time goes in v6:
time: 130 us; the launch traced here: 129 us
  Pallas kernels  125 us (96%)
  local copies, waits for them, and re-layouts  3.72 us (3%)
    pallas_call x1, Pallas kernels, tile_rows(): pl.pallas_call(tile_kernel, out_shape=(jax.ShapeDtypeStruct((2 * PAIRS, W...  64.2 us
    pallas_call x1, Pallas kernels, reduce_rows(): pl.pallas_call(reduce_kernel, out_shape=jax.ShapeDtypeStruct((STACKS_DEV,...  48.7 us
    pallas_call x1, Pallas kernels, place_rows(): pl.pallas_call(place_kernel, out_shape=jax.ShapeDtypeStruct((2 * rows_out...  6.6 us
    pallas_call x1, Pallas kernels, whiten(): pl.pallas_call(whiten_kernel, out_shape=jax.ShapeDtypeStruct((CB, GROUPS...  5.1 us
    reshape x1, local copies, waits for them, and re-layouts, whiten(): spectra.reshape(4, CB, 2 * F)  3.28 us

profile of v6, /device:TPU:4, one launch (start us, length us, event | category | flops | bytes accessed | tf_op | source)
XLA Modules:
  0.0 129.1 jit_solution(18387436090059913679)
XLA Ops:
  0.0 3.3 %reshape.12.x_ref = bf16[4,64,4096]{2,1,0:T(8,128)(2,1)S(1)} reshape(bf16[4,64,2,2048]{3,2,1,0:T(2,128)(2,1)} %param.5) | data formatting | bytes 4194304 | tf_op jit(solution)/shard_map/reshape | solution.py:83
  3.3 0.0 copy-start
  3.3 0.0 copy-start.1
  3.3 0.0 copy-start.2
  3.3 0.0 copy-start.3
  3.3 5.1 %whiten.1.own_ref = bf16[64,16384]{1,0:T(8,128)(2,1)S(1)} custom-call(bf16[4,64,4096]{2,1,0:T(8,128)(2,1)S(1)} %reshape.12.x_ref), custom_call_target="tpu_custom_call" | custom-call | flops 20000000 | bytes 4194304 | tf_op jit(solution)/shard_map/whiten/pallas_call | solution.py:75
  8.4 0.0 copy-done
  8.5 0.0 copy-done.1
  8.5 0.0 copy-done.2
  8.5 0.0 copy-done.3
  8.5 64.2 %tiles.1 = (f32[8192,128]{1,0:T(8,128)S(1)}, s32[1,4096]{1,0:T(1,128)S(1)}, s32[128,128]{1,0:T(8,128)S(1)}) custom-call(bf16[64,16384]{1,0:T(8,128)(2,1)S(1)} %whiten.1.own_ref, bf16[272,2048]{1,0:T(8,128)(2,1)S(1)} %copy-done.2, bf16[256,2048]{1,0:T(8,128)(2,1)S(1)} %copy-done.3, s32[1,4096]{1,0:T(1,128)S(1)} %bitcast.5, s32[1,4096]{1,0:T(1,128)S(1)} %bitcast.6), custom_call_target="tpu_custom_call" | custom-call | flops 24999999488 | bytes 16777216 | tf_op jit(solution)/shard_map/tiles/pallas_call | solution.py:296
  72.7 6.6 %place.1.rows_ref = bf16[16384,128]{1,0:T(8,128)(2,1)S(1)} custom-call(s32[4096]{0:T(1024)S(1)} %bitcast.4, f32[8192,128]{1,0:T(8,128)S(1)} %get-tuple-element.9.rows), custom_call_target="tpu_custom_call" | custom-call | tf_op jit(solution)/shard_map/place/pallas_call | solution.py:355
  79.3 48.7 %reduce_rows.1 = f32[128,256]{1,0:T(8,128)S(1)} custom-call(bf16[16384,128]{1,0:T(8,128)(2,1)S(1)} %place.1.rows_ref, s32[128,128]{1,0:T(8,128)S(1)} %get-tuple-element.10.slots_ref), custom_call_target="tpu_custom_call" | custom-call | flops 2000000000 | bytes 8388608 | tf_op jit(solution)/shard_map/reduce_rows/pallas_call | solution.py:546
  127.9 0.1 slice.13
  128.0 0.2 reverse.2
  128.3 0.1 slice.15
  128.4 0.7 fusion
  (1 shorter events, 0.0 us)
Async XLA Ops:
  3.3 5.2 %copy-start = (s32[4096,1]{0,1:T(1,128)S(1)}, s32[4096,1]{0,1:T(1,128)}, u32[]{:S(2)}) copy-start(s32[4096,1]{0,1:T(1,128)} %param.6) | copy-start | bytes 49156
  3.3 5.2 %copy-start.1 = (s32[4096]{0:T(1024)S(1)}, s32[4096]{0:T(1024)}, u32[]{:S(2)}) copy-start(s32[4096]{0:T(1024)} %param.7) | copy-start | bytes 49156
  3.3 5.2 %copy-start.2 = (bf16[272,2048]{1,0:T(8,128)(2,1)S(1)}, bf16[272,2048]{1,0:T(8,128)(2,1)}, u32[]{:S(2)}) copy-start(bf16[272,2048]{1,0:T(8,128)(2,1)} %constant.10.clone.cos_ref) | copy-start | bytes 3342340
  3.3 5.2 %copy-start.3 = (bf16[256,2048]{1,0:T(8,128)(2,1)S(1)}, bf16[256,2048]{1,0:T(8,128)(2,1)}, u32[]{:S(2)}) copy-start(bf16[256,2048]{1,0:T(8,128)(2,1)} %constant.11.clone.sin_ref) | copy-start | bytes 3145732
